TPU v7x, 256 devices: a whole 4x4x8 slice. The times are simulated.
256 devices in a mesh: branch: 2 (over core), seq: 8 (over y, x_lo), dp: 16 (over x_hi, z).
Axes of the slice: x: 4 (x_hi: 2, x_lo: 2; x = x_hi * 2 + x_lo), y: 4, z: 8, core: 2. Of those that a mesh axis runs over, the one named last changes fastest.
Arguments:
- context: bfloat16 [16, 1024, 5120], P('dp', 'seq', 'branch'), may hold values from -6 to 6
- main_stream: bfloat16 [16, 1024, 5120], P('dp', 'seq'), may hold values from -6 to 6
- cell_order: int32 [16, 1024], P('dp', 'seq'), may hold values from 0 to 1023, each once within a row
- modulation: float32 [16, 2, 5120], P('dp'), may hold values from -3 to 3
- hint_weight: bfloat16 [5120, 5120], P(('branch', 'dp'), 'seq'), may hold values from -0.078125 to 0.078125
- hint_bias: float32 [5120], P('seq'), may hold values from -3 to 3
- weights: bfloat16 [2, 5120, 5120], P('branch', 'dp', 'seq'), may hold values from -2 to 2
- biases: float32 [2, 5120], P('branch', 'seq'), may hold values from -3 to 3
- norm_gains: float32 [2, 5120], P('branch', 'seq'), may hold values from 0.25 to 1.75
Outputs:
- projections: bfloat16 [2, 16, 1024, 5120], P('branch', 'dp', None, 'seq')
- main_next: bfloat16 [16, 1024, 5120], P('dp', 'seq', 'branch')
Inputs may be any that keep to these rules, and one draw needn't show every extreme that they name: `cell_order`: each row lists every one of the 1024 cells of the window once.
All inputs are finite; a program needn't handle non-finite values.
Results may differ from a plain program's by a relative error of at most 0.006.
Values may be sent and summed in bfloat16 or wider, within the bound.
No kernel may reach another device: no remote copies, remote signals or barrier semaphores. Data moves between devices by JAX's collectives and lax.ppermute only.
A program may use at most 128 MiB of HBM per device.

v0:
```python
import jax
import jax.numpy as jnp
from jax import lax
from jax.sharding import PartitionSpec as P

HEAD = 128
TILE_H = 8
TILE_W = 16


norm_eps = 1e-06


def modulate(token_rows, shift_scale):
    values = token_rows.astype(jnp.float32)
    average = jnp.mean(values, axis=-1, keepdims=True)
    centered = values - average
    variance = jnp.mean(centered * centered, axis=-1, keepdims=True)
    normed = centered * lax.rsqrt(variance + norm_eps)
    return (normed * (1.0 + shift_scale[1]) + shift_scale[0]).astype(jnp.bfloat16)


def rope_tables(cell_ids):
    half_head = HEAD // 2
    sixth_head = HEAD // 6
    frame_pairs = half_head - 2 * sixth_head
    pair_index = jnp.arange(half_head, dtype=jnp.int32)
    in_frame = pair_index < frame_pairs
    in_height = jnp.logical_and(pair_index >= frame_pairs, pair_index < frame_pairs + sixth_head)
    local_index = jnp.where(
        in_frame,
        pair_index,
        jnp.where(in_height, pair_index - frame_pairs, pair_index - frame_pairs - sixth_head),
    )
    section = jnp.where(in_frame, frame_pairs, sixth_head)
    frequency = jnp.power(10000.0, -local_index.astype(jnp.float32) / section.astype(jnp.float32))
    frame_ids = cell_ids // (TILE_H * TILE_W)
    row_ids = cell_ids // TILE_W % TILE_H
    col_ids = cell_ids % TILE_W
    position = jnp.where(
        in_frame[None, :],
        frame_ids[:, None],
        jnp.where(in_height[None, :], row_ids[:, None], col_ids[:, None]),
    )
    angles = position.astype(jnp.float32) * frequency[None, :]
    return (jnp.cos(angles), jnp.sin(angles))


def rotate(values, cosine, sine_tab):
    num_rows, features = values.shape
    paired = values.reshape(num_rows, features // HEAD, HEAD // 2, 2)
    even_part = paired[..., 0]
    odd_part = paired[..., 1]
    cos_wide = cosine[:, None, :]
    sin_wide = sine_tab[:, None, :]
    turned = jnp.stack(
        [even_part * cos_wide - odd_part * sin_wide, even_part * sin_wide + odd_part * cos_wide],
        axis=-1,
    )
    return turned.reshape(num_rows, features)


def on_device(
    context,
    main_stream,
    cell_order,
    modulation,
    hint_weight,
    hint_bias,
    weights,
    biases,
    norm_gains,
):
    context_half = context[0]
    main_rows = main_stream[0]
    local_ids = cell_order[0]
    shift_scale = modulation[0]
    branch_at = lax.axis_index("branch")
    features = main_rows.shape[1]
    context_all = lax.all_gather(context_half, "seq", axis=0, tiled=True)
    hint_block = lax.all_gather(hint_weight, "dp", axis=0, tiled=True)
    partial_hint = jnp.dot(context_all, hint_block, preferred_element_type=jnp.float32)
    summed = lax.psum(partial_hint, "branch")
    hint_cols = (summed + hint_bias[None, :]).astype(jnp.bfloat16)
    hint = lax.all_to_all(hint_cols, "seq", split_axis=0, concat_axis=1, tiled=True)
    mixed = (main_rows.astype(jnp.float32) + hint.astype(jnp.float32)).astype(jnp.bfloat16)
    normed = modulate(mixed, shift_scale)
    slot_weight = weights[0]
    all_rows, cell_ids = (
        lax.all_gather(normed, "seq", axis=0, tiled=True),
        lax.all_gather(local_ids, "seq", axis=0, tiled=True),
    )
    full_weight = lax.all_gather(slot_weight, "dp", axis=0, tiled=True)
    projected = jnp.dot(all_rows, full_weight, preferred_element_type=jnp.float32)
    projected = projected + biases[0][None, :]
    squares = jnp.sum(projected * projected, axis=1)
    summed_sq = lax.psum(squares, "seq")
    inv_rms = lax.rsqrt(summed_sq / features + norm_eps)
    cosine, sine_tab = rope_tables(cell_ids)
    scaled = projected * inv_rms[:, None] * norm_gains[0][None, :]
    rotated = rotate(scaled, cosine, sine_tab).astype(jnp.bfloat16)
    half_width = features // 2
    main_next = lax.dynamic_slice_in_dim(mixed, branch_at * half_width, half_width, 1)
    return (rotated[None, None], main_next[None])


def solution(mesh):
    placed = (
        P("dp", "seq", "branch"),
        P("dp", "seq", None),
        P("dp", "seq"),
        P("dp", None, None),
        P(("branch", "dp"), "seq"),
        P("seq"),
        P("branch", "dp", "seq"),
        P("branch", "seq"),
        P("branch", "seq"),
    )
    return jax.shard_map(
        on_device,
        mesh=mesh,
        in_specs=placed,
        out_specs=(P("branch", "dp", None, "seq"), P("dp", "seq", "branch")),
        check_vma=False,
    )
```

profile of v0, /device:TPU:1, one launch (start us, length us, event | category | flops | bytes accessed | tf_op | source)
XLA Modules:
  0.0 644.2 jit_solution(12022645927925907002)
XLA Ops:
  7.2 0.0 all-gather.8.cloned.1.call-start
  7.2 0.7 all-gather.8.cloned.1.call-update
  7.9 0.0 all-gather.12.cloned.1.call-start
  7.9 0.7 all-gather.12.cloned.1.call-update
  8.6 0.0 all-reduce.2.cloned.1.call-start
  8.7 96.2 %all-gather.8.cloned.1.call-done = bf16[2560,640]{1,0:T(8,128)(2,1)} async-done(((bf16[160,640]{1,0:T(8,128)(2,1)}), bf16[2560,640]{1,0:T(8,128)(2,1)}) %all-gather.8.cloned.1.call-update) | async-done | bytes 3276816 | tf_op jit(solution)/shard_map/all_gather | solution.py:81
  104.9 114.1 %all-gather.12.cloned.1.call-done = bf16[1,1024,2560]{2,1,0:T(8,128)(2,1)} async-done(((bf16[1,128,2560]{2,1,0:T(8,128)(2,1)}), bf16[1,1024,2560]{2,1,0:T(8,128)(2,1)}) %all-gather.12.cloned.1.call-update) | async-done | bytes 5242896 | tf_op jit(solution)/shard_map/all_gather | solution.py:80
  219.0 9.2 %fusion.2 = f32[1024,640]{1,0:T(8,128)} fusion(bf16[2560,640]{1,0:T(8,128)(2,1)} %all-gather.8.cloned.1.call-done, bf16[1,1024,2560]{2,1,0:T(8,128)(2,1)} %all-gather.12.cloned.1.call-done), kind=kOutput, calls=%fused_computation.2 | convolution fusion | flops 3355443200 | bytes 11141120 | tf_op jit(solution)/shard_map/dot_general | solution.py:82
  228.2 0.0 copy-start.2
  228.2 0.0 all-reduce.2.cloned.1.call-update
  228.2 0.0 all-gather.14.cloned.1.call-start
  228.2 0.5 all-gather.14.cloned.1.call-update
  228.8 0.0 copy-start.1
  228.8 33.9 %all-reduce.2.cloned.1.call-done = f32[1024,640]{1,0:T(8,128)} async-done(((f32[1024,640]{1,0:T(8,128)}), f32[1024,640]{1,0:T(8,128)}) %all-reduce.2.cloned.1.call-update) | async-done | bytes 2621456 | tf_op jit(solution)/shard_map/psum | solution.py:83
  262.7 0.0 copy-done.2
  262.7 3.0 add_convert_fusion
  265.6 4.6 all-to-all-start
  270.3 0.0 all-gather.10.cloned.1.call-start
  270.3 0.0 copy-done.1
  270.4 22.5 %all-to-all-done = bf16[8,128,640]{2,1,0:T(8,128)(2,1)S(1)} async-done(((bf16[8,128,640]{2,1,0:T(8,128)(2,1)}), bf16[8,128,640]{2,1,0:T(8,128)(2,1)S(1)}, u32[]{:S(2)}, u32[]{:S(2)}) %all-to-all-start) | async-done | bytes 1310752 | tf_op jit(solution)/shard_map/all_to_all | solution.py:85
  292.8 0.2 convert_bitcast_fusion
  293.0 0.0 copy-start
  293.0 0.3 copy.15
  293.3 1.0 copy-done
  294.3 0.4 convert_reduce_fusion
  294.8 0.0 copy-start.3
  294.8 0.0 copy-start.4
  294.8 0.0 copy-start.5
  294.8 0.5 fusion.6
  295.3 1.6 fusion.9
  297.0 0.0 all-gather.10.cloned.1.call-update
  297.0 0.0 copy-done.3
  297.0 0.0 copy-done.4
  297.1 0.0 copy-done.5
  297.1 12.0 %all-gather.2 = s32[1,1024]{1,0:T(1,128)S(1)} all-gather(s32[1,128]{1,0:T(1,128)S(1)} %copy-done.5), channel_id=4, replica_groups=mesh['branch'=2,'seq'=8,'dp'=16] {'seq'}, dimensions={1}, use_global_device_ids=true | all-gather | bytes 4608 | tf_op jit(solution)/shard_map/all_gather | solution.py:91
  309.2 1.0 fusion.12
  310.2 0.9 dynamic-slice_bitcast_fusion
  311.1 76.9 %all-gather.14.cloned.1.call-done = bf16[1,5120,640]{2,1,0:T(8,128)(2,1)} async-done(((bf16[1,320,640]{2,1,0:T(8,128)(2,1)}), bf16[1,5120,640]{2,1,0:T(8,128)(2,1)}) %all-gather.14.cloned.1.call-update) | async-done | bytes 6553616 | tf_op jit(solution)/shard_map/all_gather | solution.py:93
  388.0 210.0 %all-gather.10.cloned.1.call-done = bf16[1024,5120]{1,0:T(8,128)(2,1)} async-done(((bf16[128,5120]{1,0:T(8,128)(2,1)}), bf16[1024,5120]{1,0:T(8,128)(2,1)}) %all-gather.10.cloned.1.call-update) | async-done | bytes 10485776 | tf_op jit(solution)/shard_map/all_gather | solution.py:90
  598.0 11.7 %multiply_reduce_fusion = (f32[1024]{0:T(1024)S(1)}, f32[1024,640]{0,1:T(8,128)S(1)}) fusion(f32[640]{0:T(1024)S(1)} %reduce, bf16[1024,5120]{1,0:T(8,128)(2,1)} %all-gather.10.cloned.1.call-done, bf16[1,5120,640]{2,1,0:T(8,128)(2,1)} %all-gather.14.cloned.1.call-done), kind=kOutput, calls=%fused_computation.16 | convolution fusion | flops 6712851456 | bytes 19667456 | tf_op jit(solution)/shard_map/dot_general | solution.py:94
  609.7 14.3 %psum.15 = f32[1024]{0:T(1024)S(1)} all-reduce(f32[1024]{0:T(1024)S(1)} %get-tuple-element.15), channel_id=1, replica_groups=mesh['branch'=2,'seq'=8,'dp'=16] {'seq'}, use_global_device_ids=true, to_apply=%region_4.0 | all-reduce | flops 1024 | bytes 8192 | tf_op jit(solution)/shard_map/psum | solution.py:97
  624.0 1.9 multiply_multiply_fusion
  625.9 3.2 reshape.211
  629.2 3.6 subtract_convert_fusion
  632.7 3.0 pad_maximum_fusion
  635.7 0.5 convert_element_type.74
  636.3 1.4 copy.14
  (9 shorter events, 0.1 us)
Async XLA Ops:
  7.2 97.7 %all-gather.8.cloned.1.call-start = ((), (), s32[]{:S(2)}) async-start(), calls=%async_computation.1 | async-start | bytes 3481600 | tf_op jit(solution)/shard_map/all_gather | solution.py:81
  7.9 211.1 %all-gather.12.cloned.1.call-start = ((), (), s32[]{:S(2)}) async-start(), calls=%async_computation.4 | async-start | bytes 5898240 | tf_op jit(solution)/shard_map/all_gather | solution.py:80
  8.6 254.0 %all-reduce.2.cloned.1.call-start = ((), (), s32[]{:S(2)}) async-start(), calls=%async_computation.2 | async-start | bytes 5242880 | tf_op jit(solution)/shard_map/psum | solution.py:83
  228.2 34.5 %copy-start.2 = (f32[640]{0:T(1024)S(1)}, f32[640]{0:T(1024)}, u32[]{:S(2)}) copy-start(f32[640]{0:T(1024)} %param.14) | copy-start | bytes 7684
  228.2 159.8 %all-gather.14.cloned.1.call-start = ((), (), s32[]{:S(2)}) async-start(), calls=%async_computation.5 | async-start | bytes 6963200 | tf_op jit(solution)/shard_map/all_gather | solution.py:93
  228.8 41.6 %copy-start.1 = (f32[1,2,5120]{2,1,0:T(2,128)S(1)}, f32[1,2,5120]{2,1,0:T(2,128)}, u32[]{:S(2)}) copy-start(f32[1,2,5120]{2,1,0:T(2,128)} %param.12) | copy-start | bytes 122884
  265.6 27.2 %all-to-all-start = ((bf16[8,128,640]{2,1,0:T(8,128)(2,1)}), bf16[8,128,640]{2,1,0:T(8,128)(2,1)S(1)}, u32[]{:S(2)}, u32[]{:S(2)}) async-start(bf16[8,128,640]{2,1,0:T(8,128)(2,1)} %bitcast.2), calls=%async_computation | async-start | bytes 2621440 | tf_op jit(solution)/shard_map/all_to_all | solution.py:85
  270.3 327.7 %all-gather.10.cloned.1.call-start = ((), (), s32[]{:S(2)}) async-start(), calls=%async_computation.3 | async-start | bytes 11796480 | tf_op jit(solution)/shard_map/all_gather | solution.py:90
  293.0 1.3 copy-start
  294.8 2.2 copy-start.3
  294.8 2.2 copy-start.4
  294.8 2.3 copy-start.5
Sparse Core Ops, SparseCore 0:
  10.6 94.2 all-gather.7
  106.6 112.2 all-gather.11
  228.3 34.2 all-reduce.1
  265.4 122.4 all-gather.13
  390.3 207.6 all-gather.9
where the time goes:
time: 648 us; the launch traced here: 644 us
  waiting for transfers between devices  555 us (86%)
  blocking collectives  26.4 us (4%)
  matrix products  20.9 us (3%)
  other arithmetic  15.3 us (2%)
  between operations  14 us (2%)
  local copies, waits for them, and re-layouts  7.45 us (1%)
    all_gather x1, waiting for transfers between devices, on_device(): lax.all_gather(normed, 'seq', axis=0, tiled=True)  210 us
    all_gather x1, waiting for transfers between devices, on_device(): context_all = lax.all_gather(context_half, 'seq', axis=0, tiled=True)  114 us
    all_gather x1, waiting for transfers between devices, on_device(): hint_block = lax.all_gather(hint_weight, 'dp', axis=0, tiled=True)  96.2 us
    all_gather x1, waiting for transfers between devices, on_device(): full_weight = lax.all_gather(slot_weight, 'dp', axis=0, tiled=True)  76.9 us
    psum x1, waiting for transfers between devices, on_device(): summed = lax.psum(partial_hint, 'branch')  33.9 us
    all_to_all x1, waiting for transfers between devices, on_device(): lax.all_to_all(hint_cols, 'seq', split_axis=0, concat_axis=1, tiled=True)  22.5 us
    psum x1, blocking collectives, on_device(): summed_sq = lax.psum(squares, 'seq')  14.3 us
  transfers between devices with their start and end apart: 6, of which 6 were waited for; matrix products, arithmetic and copies ran while one was open for 1% of the time, Pallas kernels for 0%

commit v1 on v0

v1 whole, which is shorter than its diff:
```python
import functools

import jax
import jax.numpy as jnp
from jax import lax
from jax.experimental import pallas as pl
from jax.experimental.pallas import tpu as pltpu
from jax.sharding import PartitionSpec as P

HEAD = 128
TILE_H = 8
TILE_W = 16
norm_eps = 1e-06

F32 = jnp.float32
BF16 = jnp.bfloat16

NY, NX, NH, NZ = 4, 2, 2, 8
NS = NY * NX
SWAP = [(0, 1), (1, 0)]
REL = [(0, 0), (-1, 0), (1, 0), (0, 1), (2, 0), (1, 1), (-1, 1), (2, 1)]
Z_GROUPS = [[hh * NZ + z for z in range(NZ)] for hh in range(NH)]
MIB = 1024 * 1024

HBM = pl.BlockSpec(memory_space=pltpu.HBM)
WHOLE = pl.BlockSpec(memory_space=pltpu.VMEM)
SMALL = pl.CostEstimate(flops=1, bytes_accessed=1, transcendentals=0)
SCALARS = pl.BlockSpec(memory_space=pltpu.SMEM)


def seq_pairs(dy, dx):
    return [(s, ((s // NX + dy) % NY) * NX + (s % NX ^ dx)) for s in range(NS)]


def dp_pairs(dh, dz):
    return [(d, (d // NZ ^ dh) * NZ + (d % NZ + dz) % NZ) for d in range(NH * NZ)]


def seq_send(x, dy, dx):
    return lax.ppermute(x, "seq", seq_pairs(dy, dx))


def dp_send(x, dh, dz):
    return lax.ppermute(x, "dp", dp_pairs(dh, dz))


def core_swap(x):
    return lax.ppermute(x, "branch", SWAP)


def thirds(rows):
    unit = rows // NS
    return 3 * unit, 5 * unit


def after(value, *earlier):
    return lax.optimization_barrier((value, earlier))[0]


def cat(*parts):
    return jnp.concatenate(parts, 0)


def join_kernel(a_ref, b_ref, out_ref):
    half = a_ref.shape[0]
    out_ref[:half, :] = a_ref[...]
    out_ref[half:, :] = b_ref[...]


def join(a, b):
    return pl.pallas_call(
        join_kernel,
        out_shape=jax.ShapeDtypeStruct((2 * a.shape[0], a.shape[1]), a.dtype),
        in_specs=[WHOLE] * 2,
        out_specs=WHOLE,
        cost_estimate=SMALL,
        name="join",
    )(a, b)


def relay_context(own, beside_first, beside_second, beside_third):
    half = own.shape[0] // 2
    back, ahead, extra = lax.optimization_barrier(
        (seq_send(own, 1, 0), seq_send(own, -1, 0), beside_first)
    )
    up, down, beside, more = lax.optimization_barrier(
        (
            seq_send(back[:half], 1, 0),
            seq_send(ahead[half:], -1, 0),
            seq_send(after(own, back), 0, 1),
            beside_second(extra),
        )
    )
    far = join(up, down)
    ahead_beside, back_beside, far_beside, extra = lax.optimization_barrier(
        (seq_send(beside, -1, 0), seq_send(beside, 1, 0), seq_send(far, 0, 1), beside_third(beside))
    )
    return [own, back, ahead, beside, far, ahead_beside, back_beside, far_beside], more, extra


def hint_kernel(rows, where_ref, weight_ref, *refs):
    blocks = refs[:NS]
    other_ref, mine_ref, ctx, wgt, sem = refs[NS:]
    half_rows = rows // 2
    depth = weight_ref.shape[1] // NH
    mine = where_ref[8]
    copies = []

    def copy(src, dst):
        c = pltpu.make_async_copy(src, dst, sem.at[len(copies)])
        c.start()
        copies.append(c)

    def tokens(half, slot):
        for i, block in enumerate(blocks):
            src = pl.ds(pl.multiple_of(half * half_rows, 16), half_rows)
            copy(block.at[src], ctx.at[slot, pl.ds(pl.multiple_of(where_ref[i] * half_rows, 16), half_rows)])

    tokens(1 - mine, 0)
    for h in range(NH):
        for z in range(NZ):
            copy(weight_ref.at[z, pl.ds(h * depth, depth)], wgt.at[pl.ds((h * NZ + z) * depth, depth)])
    tokens(mine, 1)
    for c in copies[: NS + NH * NZ]:
        c.wait()
    other_ref[...] = jnp.dot(ctx[0], wgt[...], preferred_element_type=F32)
    for c in copies[NS + NH * NZ :]:
        c.wait()
    mine_ref[...] = jnp.dot(ctx[1], wgt[...], preferred_element_type=F32)


def hint_matmul(where, blocks, weight):
    rows, features = blocks[0].shape
    columns = weight.shape[2]
    half = NS * rows // 2
    return pl.pallas_call(
        functools.partial(hint_kernel, rows),
        out_shape=[jax.ShapeDtypeStruct((half, columns), F32)] * 2,
        in_specs=[SCALARS] + [HBM] * (1 + NS),
        out_specs=[WHOLE] * 2,
        scratch_shapes=[
            pltpu.VMEM((2, half, features), BF16),
            pltpu.VMEM((features, columns), BF16),
            pltpu.SemaphoreType.DMA((2 * NS + NH * NZ,)),
        ],
        compiler_params=pltpu.CompilerParams(vmem_limit_bytes=60 * MIB),
        cost_estimate=SMALL,
        name="hint",
    )(where, weight, *blocks)


def mix_kernel(keep_ref, got_ref, main_ref, bias_ref, cell_ref, mixed_ref, small_ref):
    rows = keep_ref.shape[0]
    lines = rows // 128
    hint = (keep_ref[...] + got_ref[...] + bias_ref[...]).astype(BF16)
    mixed = (main_ref[...].astype(F32) + hint.astype(F32)).astype(BF16)
    mixed_ref[...] = mixed
    values = mixed.astype(F32)
    average = jnp.mean(values, axis=-1, keepdims=True)
    centered = values - average
    spread = jnp.sum(centered * centered, axis=-1, keepdims=True)
    lane = lax.broadcasted_iota(jnp.int32, (rows, 128), 1)
    both = jnp.where(lane == 0, average, spread).T
    cells = jnp.broadcast_to(cell_ref[...].astype(F32), (8, 128))
    for d in range(NS):
        for r in range(2):
            for k in range(lines):
                small_ref[d, r * lines + k : r * lines + k + 1, :] = both[r : r + 1, k * 128 : (k + 1) * 128]
        small_ref[d, 2 * lines :, :] = cells


def mix(keep, got, main_cols, bias, cells):
    rows, columns = keep.shape
    return pl.pallas_call(
        mix_kernel,
        out_shape=[
            jax.ShapeDtypeStruct((rows, columns), BF16),
            jax.ShapeDtypeStruct((NS, 2 * rows // 128 + 8, 128), F32),
        ],
        compiler_params=pltpu.CompilerParams(vmem_limit_bytes=16 * MIB),
        cost_estimate=SMALL,
        name="mix",
    )(keep, got, main_cols, bias, cells)


def norm_kernel(rows, width, order, pieces, where_ref, norm_ref, mod_ref, *refs):
    mean, rstd, xs, sem = refs[-4:]
    normed_ref, next_ref = refs[-6:-4]
    arrays = refs[:-6]
    copies = []
    for k, (block, array, first, lo, hi) in enumerate(pieces):
        src, dst = arrays[array].at[pl.ds(first, hi - lo)], xs.at[order.index(block), pl.ds(lo, hi - lo)]
        c = pltpu.make_async_copy(src, dst, sem.at[k])
        c.start()
        copies.append(c)
    mean[...] = jnp.broadcast_to(norm_ref[0:1, :], (128, rows)).T
    rstd[...] = jnp.broadcast_to(norm_ref[1:2, :], (128, rows)).T
    for c in copies:
        c.wait()
    step = 128
    tokens = rows // NS
    me = pl.ds(pl.multiple_of(where_ref[9] * tokens, 16), tokens)
    for j, block in enumerate(order):
        s = where_ref[block]
        shift, scale = mod_ref[s, 0:1, :], 1.0 + mod_ref[s, 1:2, :]

        def body(i, _, j=j, shift=shift, scale=scale):
            at = pl.ds(pl.multiple_of(i * step, 16), step)
            into = pl.ds(pl.multiple_of(j * rows + i * step, 16), step)
            average, root = mean[at, :], rstd[at, :]
            for a in range(width // 128):
                lanes = slice(a * 128, (a + 1) * 128)
                values = (xs[j, at, lanes].astype(F32) - average) * root
                normed_ref[into, lanes] = (values * scale[:, lanes] + shift[:, lanes]).astype(BF16)
            return 0

        lax.fori_loop(0, rows // step, body, 0)
        next_ref[j] = xs[j, me, :]


def norm(where, norm_rows, mod, arrays, pieces):
    order = sorted({piece[0] for piece in pieces})
    rows, width = norm_rows.shape[1], mod.shape[2]
    tokens = rows // NS
    return pl.pallas_call(
        functools.partial(norm_kernel, rows, width, order, pieces),
        out_shape=[
            jax.ShapeDtypeStruct((len(order) * rows, width), BF16),
            jax.ShapeDtypeStruct((len(order), tokens, width), BF16),
        ],
        in_specs=[SCALARS, WHOLE, WHOLE] + [HBM] * len(arrays),
        out_specs=[WHOLE] * 2,
        scratch_shapes=[
            pltpu.VMEM((rows, 128), F32),
            pltpu.VMEM((rows, 128), F32),
            pltpu.VMEM((len(order), rows, width), BF16),
            pltpu.SemaphoreType.DMA((len(pieces),)),
        ],
        compiler_params=pltpu.CompilerParams(vmem_limit_bytes=60 * MIB),
        cost_estimate=SMALL,
        name="norm",
    )(where, norm_rows, mod, *arrays)


def next_kernel(where_ref, first_ref, second_ref, *refs):
    pieces, out_ref, whole = refs[:-2], refs[-2], refs[-1]
    tokens, width = first_ref.shape[1:]

    def put(block, part):
        s = where_ref[block]
        out_ref[s // NY, :, pl.ds(pl.multiple_of((s % NY) * width, 128), width)] = part

    count = first_ref.shape[0]
    for j in range(count):
        put(j, first_ref[j])
    for j in range(second_ref.shape[0]):
        put(count + j, second_ref[j])
    at = 0
    for ref in pieces:
        whole[at : at + ref.shape[0], :] = ref[...]
        at += ref.shape[0]
    put(NS - 1, whole[pl.ds(pl.multiple_of(where_ref[9] * tokens, 16), tokens), :])


def next_rows(where, first, second, last):
    tokens, width = first.shape[1:]
    return pl.pallas_call(
        next_kernel,
        out_shape=jax.ShapeDtypeStruct((2, tokens, NY * width), BF16),
        in_specs=[SCALARS] + [WHOLE] * (2 + len(last)),
        out_specs=WHOLE,
        scratch_shapes=[pltpu.VMEM((sum(piece.shape[0] for piece in last), width), BF16)],
        compiler_params=pltpu.CompilerParams(vmem_limit_bytes=16 * MIB),
        cost_estimate=SMALL,
        name="next_rows",
    )(where, first, second, *last)


def project_kernel(counts, cuts, where_ref, *refs):
    sets = len(counts) + len(cuts) - 2
    mine, other = refs[:sets], refs[sets : 2 * sets]
    w_ref, bias_ref, norm_ref, norm_other_ref, mod_ref, out_ref, squares_ref = refs[2 * sets : 2 * sets + 7]
    xs, wgt, raw, mean, rstd, sem_x, sem_w = refs[2 * sets + 7 :]
    rows = out_ref.shape[0] // 2
    width = wgt.shape[0] // NS
    deep = width // 2
    copies = []
    i = 0
    for count, a, b in zip(counts, mine, other):
        for j in range(count):
            src, lanes = pl.ds(j * rows, rows), pl.ds(i * width, width)
            s = where_ref[i]
            z, h = lax.rem(2 * s, NZ), lax.div(2 * s, NZ)
            from_w = pl.ds(pl.multiple_of(h * deep, 16), deep)
            copies.append(
                [
                    pltpu.make_async_copy(w_ref.at[z, from_w], wgt.at[pl.ds(i * width, deep)], sem_w.at[i, 0]),
                    pltpu.make_async_copy(
                        w_ref.at[z + 1, from_w], wgt.at[pl.ds(i * width + deep, deep)], sem_w.at[i, 1]
                    ),
                ]
            )
            if i < NS - 1:
                copies[i] += [
                    pltpu.make_async_copy(a.at[src], xs.at[pl.ds(0, rows), lanes], sem_x.at[2 * i]),
                    pltpu.make_async_copy(b.at[src], xs.at[pl.ds(rows, rows), lanes], sem_x.at[2 * i + 1]),
                ]
            i += 1
    raw_copies = [
        pltpu.make_async_copy(
            refs[side * sets + len(counts) - 1 + k],
            raw.at[pl.ds(side * rows + cuts[k], cuts[k + 1] - cuts[k])],
            sem_x.at[2 * NS + side * (len(cuts) - 1) + k],
        )
        for side in range(2)
        for k in range(len(cuts) - 1)
    ]

    def start(i):
        for c in copies[i] + copies[i + 1]:
            c.start()

    start(0)
    for c in raw_copies:
        c.start()
    start(2)
    for part, ref in enumerate((norm_ref, norm_other_ref)):
        at = pl.ds(part * rows, rows)
        mean[at, :] = jnp.broadcast_to(ref[0:1, :], (128, rows)).T
        rstd[at, :] = jnp.broadcast_to(ref[1:2, :], (128, rows)).T
    s = where_ref[NS - 1]
    shift, scale = mod_ref[s, 0:1, :], 1.0 + mod_ref[s, 1:2, :]
    for i in range(0, NS, 2):
        for c in copies[i] + copies[i + 1]:
            c.wait()
        if i + 4 < NS:
            start(i + 4)
        if i == NS - 2:
            for c in raw_copies:
                c.wait()
            for a in range(width // 128):
                lanes = slice(a * 128, (a + 1) * 128)
                values = (raw[:, lanes].astype(F32) - mean[...]) * rstd[...]
                xs[:, (NS - 1) * width + a * 128 : (NS - 1) * width + (a + 1) * 128] = (
                    values * scale[:, lanes] + shift[:, lanes]
                ).astype(BF16)
        deep_lanes = pl.ds(i * width, 2 * width)
        for part in range(2):
            at = pl.ds(part * rows, rows)
            product = jnp.dot(xs[at, deep_lanes], wgt[deep_lanes, :], preferred_element_type=F32)
            if i == 0:
                out_ref[at, :] = product + bias_ref[...]
            else:
                out_ref[at, :] += product
    lane = lax.broadcasted_iota(jnp.int32, (rows, 128), 1)
    sums = []
    for part in range(2):
        values = out_ref[pl.ds(part * rows, rows), :]
        sums.append(jnp.sum(values * values, axis=-1, keepdims=True))
    both = jnp.where(lane == 0, sums[0], sums[1]).T
    lines = rows // 128
    for d in range(NS):
        for r in range(2):
            for k in range(lines):
                squares_ref[d, r * lines + k : r * lines + k + 1, :] = both[r : r + 1, k * 128 : (k + 1) * 128]


def project(where, mine, other, weight, bias, norm_rows, norm_other, mod):
    width, columns = mine[0].shape[1], weight.shape[2]
    counts = [4, 3, 1]
    rows = mine[0].shape[0] // counts[0]
    cuts = [0, *thirds(rows), rows]
    operands = [*mine, *other, weight]
    return pl.pallas_call(
        functools.partial(project_kernel, counts, cuts),
        out_shape=[
            jax.ShapeDtypeStruct((2 * rows, columns), F32),
            jax.ShapeDtypeStruct((NS, 2 * rows // 128, 128), F32),
        ],
        in_specs=[SCALARS] + [HBM] * len(operands) + [WHOLE] * 4,
        out_specs=[WHOLE] * 2,
        scratch_shapes=[
            pltpu.VMEM((2 * rows, NS * width), BF16),
            pltpu.VMEM((NS * width, columns), BF16),
            pltpu.VMEM((2 * rows, width), BF16),
            pltpu.VMEM((2 * rows, 128), F32),
            pltpu.VMEM((2 * rows, 128), F32),
            pltpu.SemaphoreType.DMA((2 * NS + 2 * len(cuts),)),
            pltpu.SemaphoreType.DMA((NS, 2)),
        ],
        compiler_params=pltpu.CompilerParams(vmem_limit_bytes=60 * MIB),
        cost_estimate=pl.CostEstimate(
            flops=4 * rows * NS * width * columns,
            bytes_accessed=2 * NS * width * (2 * rows + columns) + 8 * rows * columns,
            transcendentals=0,
        ),
        name="project",
    )(where, *operands, bias, norm_rows, norm_other, mod)


def turn_kernel(where_ref, proj_ref, gain_ref, cos_ref, sin_ref, out_ref):
    tokens, columns = out_ref.shape
    part = tokens // 2 // NS
    mine = where_ref[8]
    even = lax.broadcasted_iota(jnp.int32, (part, HEAD), 1) % 2 == 0

    def body(s, _):
        for h in range(2):
            half = mine if h == 0 else 1 - mine
            src = pl.ds(pl.multiple_of((h * NS + s) * part, 16), part)
            dst = pl.ds(pl.multiple_of((2 * s + half) * part, 16), part)
            cosine, sine = cos_ref[dst, :], sin_ref[dst, :]
            for a in range(columns // HEAD):
                lanes = slice(a * HEAD, (a + 1) * HEAD)
                value = proj_ref[src, lanes] * gain_ref[:, lanes]
                partner = jnp.where(even, pltpu.roll(value, HEAD - 1, 1), pltpu.roll(value, 1, 1))
                out_ref[dst, lanes] = value * cosine + partner * sine
        return 0

    lax.fori_loop(0, NS, body, 0)


def turn(where, proj, gain, cosine, sine):
    tokens, columns = proj.shape
    return pl.pallas_call(
        turn_kernel,
        out_shape=jax.ShapeDtypeStruct((tokens, columns), F32),
        in_specs=[SCALARS] + [WHOLE] * 4,
        out_specs=WHOLE,
        compiler_params=pltpu.CompilerParams(vmem_limit_bytes=60 * MIB),
        cost_estimate=pl.CostEstimate(flops=10 * tokens * columns, bytes_accessed=9 * tokens * columns, transcendentals=0),
        name="turn",
    )(where, proj, gain, cosine, sine)


def rope_tables(cell_ids):
    half_head = HEAD // 2
    sixth_head = HEAD // 6
    frame_pairs = half_head - 2 * sixth_head
    lane = jnp.arange(HEAD, dtype=jnp.int32)
    pair_index = lane // 2
    in_frame = pair_index < frame_pairs
    in_height = jnp.logical_and(pair_index >= frame_pairs, pair_index < frame_pairs + sixth_head)
    local_index = jnp.where(
        in_frame,
        pair_index,
        jnp.where(in_height, pair_index - frame_pairs, pair_index - frame_pairs - sixth_head),
    )
    section = jnp.where(in_frame, frame_pairs, sixth_head)
    frequency = jnp.power(10000.0, -local_index.astype(F32) / section.astype(F32))
    frame_ids = cell_ids // (TILE_H * TILE_W)
    row_ids = cell_ids // TILE_W % TILE_H
    col_ids = cell_ids % TILE_W
    position = jnp.where(
        in_frame[None, :],
        frame_ids[:, None],
        jnp.where(in_height[None, :], row_ids[:, None], col_ids[:, None]),
    )
    angles = position.astype(F32) * frequency[None, :]
    sign = jnp.where(lane % 2 == 0, -1.0, 1.0)
    return jnp.cos(angles), jnp.sin(angles) * sign[None, :]


def on_device(
    context,
    main_stream,
    cell_order,
    modulation,
    hint_weight,
    hint_bias,
    weights,
    biases,
    norm_gains,
):
    branch = lax.axis_index("branch")
    seq = lax.axis_index("seq")
    dp = lax.axis_index("dp")
    y, x = seq // NX, seq % NX
    hh = dp // NZ
    where = jnp.stack(
        [((y + dy) % NY) * NX + (x + dx) % NX for dy, dx in REL] + [branch, seq]
    ).astype(jnp.int32)

    tokens, features = main_stream.shape[1:]
    width = features // NS
    part = tokens // 2
    rows = NS * part
    lines = rows // 128

    def both_columns(own, other):
        return jnp.where(hh == 0, cat(own, other), cat(other, own))

    def along_z(both):
        return lax.all_gather(both, "dp", axis=0, axis_index_groups=Z_GROUPS)

    hint_both = both_columns(hint_weight, dp_send(hint_weight, 1, 0))
    hint_weights = along_z(hint_both)
    slot = weights[0]
    slot_other = dp_send(slot, 1, 0)

    def send_main(beside):
        half = lax.dynamic_slice_in_dim(main_stream[0], branch * part, part, 0)
        half = after(jnp.transpose(half.reshape(part, NS, width), (1, 0, 2)), beside)
        return lax.all_to_all(half, "seq", split_axis=0, concat_axis=0, tiled=True).reshape(rows, width)

    blocks, slot_both, main_cols = relay_context(
        context[0], slot_other, lambda slot_other: both_columns(slot, slot_other), send_main
    )
    weight = along_z(slot_both)

    sent, kept = hint_matmul(where, blocks, hint_weights)
    got = core_swap(sent)
    mixed, small = mix(kept, got, main_cols, hint_bias[None, :], cell_order)

    half = rows // 2
    cut_a, cut_b = thirds(rows)
    back, ahead, beside, small = lax.optimization_barrier(
        (
            seq_send(mixed, 1, 0),
            seq_send(mixed, -1, 0),
            seq_send(mixed, 0, 1),
            lax.all_to_all(small, "seq", split_axis=0, concat_axis=0, tiled=True),
        )
    )
    up = seq_send(cat(back[:half], beside[half:]), 1, 0)
    down = seq_send(cat(beside[:half], ahead[half:]), -1, 0)
    over = seq_send(cat(back[:half], ahead[half:]), 0, 1)
    means = small[:, 0:lines].reshape(NS, rows)
    spreads = small[:, lines : 2 * lines].reshape(NS, rows)
    average = jnp.mean(means, axis=0)
    apart = means - average[None, :]
    variance = (jnp.sum(spreads, axis=0) + width * jnp.sum(apart * apart, axis=0)) / features
    norm_rows = cat(average[None], lax.rsqrt(variance + norm_eps)[None], jnp.zeros((6, rows), F32))
    cells = small[:, 2 * lines].reshape(NS * tokens).astype(jnp.int32)
    mod = jnp.transpose(modulation[0].reshape(2, NS, width), (1, 0, 2))
    first, first_next = norm(
        where, norm_rows, mod, [mixed, back, ahead, beside], [(i, i, 0, 0, rows) for i in range(4)]
    )
    up, down, over = lax.optimization_barrier((up, down, over))
    first_got = core_swap(first)
    last = [
        seq_send(up[:cut_a], 0, 1),
        seq_send(cat(over[cut_a:half], up[half:cut_b]), 1, 0),
        seq_send(over[cut_b:], -1, 0),
    ]
    second, second_next = norm(
        where,
        norm_rows,
        mod,
        [up, down, over],
        [
            (4, 0, 0, 0, half),
            (4, 1, half, half, rows),
            (5, 1, 0, 0, half),
            (5, 2, half, half, rows),
            (6, 2, 0, 0, half),
            (6, 0, half, half, rows),
        ],
    )
    tables = rope_tables(after(cells, up))
    norm_other = core_swap(after(norm_rows, up))
    last, second, tables, norm_other = lax.optimization_barrier((last, second, tables, norm_other))
    second_got = core_swap(second)
    last_got = [core_swap(piece) for piece in last]
    next_half = next_rows(where, first_next, second_next, last)

    weight = after(weight, last, next_half)
    proj, squares = project(
        where, [first, second, *last], [first_got, second_got, *last_got], weight, biases, norm_rows, norm_other, mod
    )
    squares = lax.all_to_all(squares, "seq", split_axis=0, concat_axis=0, tiled=True)
    turned = turn(where, proj, norm_gains, *tables)

    next_mine = lax.dynamic_index_in_dim(next_half, branch, 0, keepdims=False)
    next_sent = lax.dynamic_index_in_dim(next_half, 1 - branch, 0, keepdims=False)
    next_got = core_swap(next_sent)
    main_next = jnp.where(branch == 0, cat(next_mine, next_got), cat(next_got, next_mine))

    squares, main_next, turned = lax.optimization_barrier((squares, main_next, turned))
    inv_rms = lax.rsqrt(jnp.sum(squares, axis=0) / features + norm_eps).reshape(2, NS, part)
    inv_rms = jnp.where(branch == 0, inv_rms, inv_rms[::-1])
    inv_rms = jnp.transpose(inv_rms, (1, 0, 2)).reshape(NS * tokens)
    rotated = (turned * inv_rms[:, None]).astype(BF16)
    return (rotated[None, None], main_next[None])


def solution(mesh):
    placed = (
        P("dp", "seq", "branch"),
        P("dp", "seq", None),
        P("dp", "seq"),
        P("dp", None, None),
        P(("branch", "dp"), "seq"),
        P("seq"),
        P("branch", "dp", "seq"),
        P("branch", "seq"),
        P("branch", "seq"),
    )
    return jax.shard_map(
        on_device,
        mesh=mesh,
        in_specs=placed,
        out_specs=(P("branch", "dp", None, "seq"), P("dp", "seq", "branch")),
        check_vma=False,
    )
```

time: 648 us -> 191 us (0.29)
  waiting for transfers between devices: 555 us -> 59.8 us
  starting transfers between devices: 4.84 us -> 50.6 us
  Pallas kernels: 0 us -> 43.4 us
  blocking collectives: 26.4 us -> 0 us
  matrix products: 20.9 us -> 0 us
    all_gather x4 -> x2, waiting for transfers between devices: 497 us -> 0.04 us  [along_z(): return lax.all_gather(both, 'dp', axis=0, axis_index_groups=Z_GROUPS)]
    pallas_call x0 -> x8, Pallas kernels: none -> 43.4 us  [the longest x1 13.9 us: project(): pl.pallas_call(functools.partial(project_kernel, counts, cuts), out_shape...]
    ppermute x0 -> x27, starting transfers between devices: none -> 39.5 us  [the longest x17 19.9 us: seq_send(): return lax.ppermute(x, 'seq', seq_pairs(dy, dx))]
    ppermute x0 -> x27, waiting for transfers between devices: none -> 34.9 us  [the longest x17 17.5 us: seq_send(): return lax.ppermute(x, 'seq', seq_pairs(dy, dx))]
    psum x1 -> x0, waiting for transfers between devices: 33.9 us -> none  [on_device(): summed = lax.psum(partial_hint, 'branch')]
    dot_general x2 -> x0, matrix products: 20.9 us -> none  [the longest x1 11.7 us: on_device(): jnp.dot(all_rows, full_weight, preferred_element_type=jnp.float32)]
    psum x1 -> x0, blocking collectives: 14.3 us -> none  [on_device(): summed_sq = lax.psum(squares, 'seq')]
    all_gather x1 -> x0, blocking collectives: 12 us -> none  [on_device(): lax.all_gather(local_ids, 'seq', axis=0, tiled=True)]
  transfers between devices with their start and end apart: 6 -> 32, of which waited for: 6 -> 15; matrix products, arithmetic and copies ran while one was open for 1% -> 7% of each run, Pallas kernels for 0% -> 23%
where the time goes in v1:
time: 191 us; the launch traced here: 190 us
  waiting for transfers between devices  59.8 us (31%)
  starting transfers between devices  50.6 us (26%)
  Pallas kernels  43.4 us (23%)
  between operations  14.6 us (8%)
  other arithmetic  13.5 us (7%)
  local copies, waits for them, and re-layouts  8.45 us (4%)
    ppermute x17, starting transfers between devices, seq_send(): return lax.ppermute(x, 'seq', seq_pairs(dy, dx))  19.9 us
    ppermute x17, waiting for transfers between devices, seq_send(): return lax.ppermute(x, 'seq', seq_pairs(dy, dx))  17.5 us
    pallas_call x1, Pallas kernels, project(): pl.pallas_call(functools.partial(project_kernel, counts, cuts), out_shape...  13.9 us
    ppermute x8, starting transfers between devices, core_swap(): return lax.ppermute(x, 'branch', SWAP)  13.2 us
    all_to_all x1, waiting for transfers between devices, on_device(): lax.all_to_all(small, 'seq', split_axis=0, concat_axis=0, tiled=True)  12.5 us
    all_to_all x1, waiting for transfers between devices, send_main(): lax.all_to_all(half, 'seq', split_axis=0, concat_axis=0, tiled=True)  12.4 us
    ppermute x2, waiting for transfers between devices, dp_send(): return lax.ppermute(x, 'dp', dp_pairs(dh, dz))  12.2 us
    pallas_call x1, Pallas kernels, hint_matmul(): pl.pallas_call(functools.partial(hint_kernel, rows), out_shape=[jax.Shape...  10.4 us
  transfers between devices with their start and end apart: 32, of which 15 were waited for; matrix products, arithmetic and copies ran while one was open for 7% of the time, Pallas kernels for 23%

profile of v1, /device:TPU:1, one launch (start us, length us, event | category | flops | bytes accessed | tf_op | source)
XLA Modules:
  0.0 190.4 jit_solution(11073567552687158717)
XLA Ops:
  7.2 3.7 %collective-permute-start = (bf16[160,640]{1,0:T(8,128)(2,1)}, bf16[160,640]{1,0:T(8,128)(2,1)S(1)}, u32[]{:S(2)}, u32[]{:S(2)}) collective-permute-start(bf16[160,640]{1,0:T(8,128)(2,1)} %param.13), channel_id=1, source_target_pairs={{0,8},{1,9},{2,10},{3,11},{4,12},{5,13},{6,14},{7,15},{8,0},{9,1},... | collective-permute-start | bytes 614408 | tf_op jit(solution)/shard_map/ppermute | solution.py:44
  10.9 4.1 %collective-permute-done = bf16[160,640]{1,0:T(8,128)(2,1)S(1)} collective-permute-done((bf16[160,640]{1,0:T(8,128)(2,1)}, bf16[160,640]{1,0:T(8,128)(2,1)S(1)}, u32[]{:S(2)}, u32[]{:S(2)}) %collective-permute-start) | collective-permute-done | bytes 204832 | tf_op jit(solution)/shard_map/ppermute | solution.py:44
  15.0 1.9 maximum_select_fusion.2
  16.9 3.7 %collective-permute-start.2 = (bf16[128,2560]{1,0:T(8,128)(2,1)}, bf16[128,2560]{1,0:T(8,128)(2,1)S(1)}, u32[]{:S(2)}, u32[]{:S(2)}) collective-permute-start(bf16[128,2560]{1,0:T(8,128)(2,1)} %bitcast.39), channel_id=1, source_target_pairs={{0,96},{16,112},{32,0},{48,16},{64,32},{80,48},{96,64},{112,80},{1... | collective-permute-start | bytes 1966088 | tf_op jit(solution)/shard_map/ppermute | solution.py:40
  20.6 2.7 %collective-permute-start.3 = (bf16[320,640]{1,0:T(8,128)(2,1)}, bf16[320,640]{1,0:T(8,128)(2,1)S(1)}, u32[]{:S(2)}, u32[]{:S(2)}) collective-permute-start(bf16[320,640]{1,0:T(8,128)(2,1)} %bitcast.44), channel_id=1, source_target_pairs={{0,8},{1,9},{2,10},{3,11},{4,12},{5,13},{6,14},{7,15},{8,0},{9,1},... | collective-permute-start | bytes 1228808 | tf_op jit(solution)/shard_map/ppermute | solution.py:44
  23.3 8.1 %collective-permute-done.3 = bf16[320,640]{1,0:T(8,128)(2,1)S(1)} collective-permute-done((bf16[320,640]{1,0:T(8,128)(2,1)}, bf16[320,640]{1,0:T(8,128)(2,1)S(1)}, u32[]{:S(2)}, u32[]{:S(2)}) %collective-permute-start.3) | collective-permute-done | bytes 409632 | tf_op jit(solution)/shard_map/ppermute | solution.py:44
  31.4 1.9 %collective-permute-done.2.refs_2_ = bf16[128,2560]{1,0:T(8,128)(2,1)S(1)} collective-permute-done((bf16[128,2560]{1,0:T(8,128)(2,1)}, bf16[128,2560]{1,0:T(8,128)(2,1)S(1)}, u32[]{:S(2)}, u32[]{:S(2)}) %collective-permute-start.2) | collective-permute-done | bytes 655392 | tf_op jit(solution)/shard_map/ppermute | solution.py:40
  33.4 3.0 %collective-permute-done.1.refs_1_ = bf16[128,2560]{1,0:T(8,128)(2,1)S(1)} collective-permute-done((bf16[128,2560]{1,0:T(8,128)(2,1)}, bf16[128,2560]{1,0:T(8,128)(2,1)S(1)}, u32[]{:S(2)}, u32[]{:S(2)}) %collective-permute-start.1) | collective-permute-done | bytes 655392 | tf_op jit(solution)/shard_map/ppermute | solution.py:40
  36.4 1.2 collective-permute-start.6
  39.1 2.7 %collective-permute-start.5 = (bf16[64,2560]{1,0:T(8,128)(2,1)}, bf16[64,2560]{1,0:T(8,128)(2,1)}, u32[]{:S(2)}, u32[]{:S(2)}) collective-permute-start(bf16[64,2560]{1,0:T(8,128)(2,1)} %slice.42), channel_id=1, source_target_pairs={{0,96},{16,112},{32,0},{48,16},{64,32},{80,48},{96,64},{112,80},{1... | collective-permute-start | bytes 983048 | tf_op jit(solution)/shard_map/ppermute | solution.py:40
  41.8 1.3 maximum_select_fusion
  43.1 3.8 %collective-permute-done.4.a_ref = bf16[64,2560]{1,0:T(8,128)(2,1)} collective-permute-done((bf16[64,2560]{1,0:T(8,128)(2,1)}, bf16[64,2560]{1,0:T(8,128)(2,1)}, u32[]{:S(2)}, u32[]{:S(2)}) %collective-permute-start.4) | collective-permute-done | bytes 327712 | tf_op jit(solution)/shard_map/ppermute | solution.py:40
  46.9 3.3 %collective-permute-done.6.refs_3_ = bf16[128,2560]{1,0:T(8,128)(2,1)} collective-permute-done((bf16[128,2560]{1,0:T(8,128)(2,1)}, bf16[128,2560]{1,0:T(8,128)(2,1)}, u32[]{:S(2)}, u32[]{:S(2)}) %collective-permute-start.6) | collective-permute-done | bytes 655392 | tf_op jit(solution)/shard_map/ppermute | solution.py:40
  50.3 2.7 %collective-permute-start.7 = (bf16[128,2560]{1,0:T(8,128)(2,1)}, bf16[128,2560]{1,0:T(8,128)(2,1)S(1)}, u32[]{:S(2)}, u32[]{:S(2)}) collective-permute-start(bf16[128,2560]{1,0:T(8,128)(2,1)} %collective-permute-done.6.refs_3_), channel_id=1, source_target_pairs={{0,96},{16,112},{32,0},{48,16},{64,32},{80,48},{96,64},{112,80},{1... | collective-permute-start | bytes 1966088 | tf_op jit(solution)/shard_map/ppermute | solution.py:40
  53.0 2.0 %join.1.refs_4_ = bf16[128,2560]{1,0:T(8,128)(2,1)} custom-call(bf16[64,2560]{1,0:T(8,128)(2,1)} %collective-permute-done.4.a_ref, bf16[64,2560]{1,0:T(8,128)(2,1)} %collective-permute-done.5.b_ref), custom_call_target="tpu_custom_call" | custom-call | flops 1 | bytes 1 | tf_op jit(solution)/shard_map/join/pallas_call | solution.py:71
  55.0 1.2 collective-permute-start.9
  56.3 0.9 copy.14
  57.2 3.5 %all-to-all-start = ((bf16[8,64,640]{2,1,0:T(8,128)(2,1)}), bf16[8,64,640]{2,1,0:T(8,128)(2,1)S(1)}, u32[]{:S(2)}, u32[]{:S(2)}) async-start(bf16[8,64,640]{2,1,0:T(8,128)(2,1)} %copy.14), calls=%async_computation | async-start | bytes 1310720 | tf_op jit(solution)/shard_map/all_to_all | solution.py:504
  61.5 12.4 %all-to-all-done = bf16[8,64,640]{2,1,0:T(8,128)(2,1)S(1)} async-done(((bf16[8,64,640]{2,1,0:T(8,128)(2,1)}), bf16[8,64,640]{2,1,0:T(8,128)(2,1)S(1)}, u32[]{:S(2)}, u32[]{:S(2)}) %all-to-all-start) | async-done | bytes 655392 | tf_op jit(solution)/shard_map/all_to_all | solution.py:504
  75.0 10.4 %hint.1 = (f32[512,640]{1,0:T(8,128)}, f32[512,640]{1,0:T(8,128)}) custom-call(s32[10]{0:T(128)} %stack.43.where_ref, bf16[8,320,640]{2,1,0:T(8,128)(2,1)} %all-gather.4.cloned.1.call-done.weight_ref, bf16[128,2560]{1,0:T(8,128)(2,1)} %bitcast.42, bf16[128,2560]{1,0:T(8,128)(2,1)} %copy-done.12, bf16[128,2560]{1,0:T(8,128)(2,1)} %copy-done.11, ...), custom_call_target="tpu_custom_call" | custom-call | flops 1 | bytes 1 | tf_op jit(solution)/shard_map/hint/pallas_call | solution.py:136
  85.3 5.5 %collective-permute-start.10 = (f32[512,640]{1,0:T(8,128)}, f32[512,640]{1,0:T(8,128)S(1)}, u32[]{:S(2)}, u32[]{:S(2)}) collective-permute-start(f32[512,640]{1,0:T(8,128)} %get-tuple-element.57), channel_id=1, source_target_pairs={{0,128},{128,0},{1,129},{129,1},{2,130},{130,2},{3,131},{131,3},{4... | collective-permute-start | bytes 3932168 | tf_op jit(solution)/shard_map/ppermute | solution.py:48
  90.8 2.9 %collective-permute-done.10.got_ref = f32[512,640]{1,0:T(8,128)S(1)} collective-permute-done((f32[512,640]{1,0:T(8,128)}, f32[512,640]{1,0:T(8,128)S(1)}, u32[]{:S(2)}, u32[]{:S(2)}) %collective-permute-start.10) | collective-permute-done | bytes 1310752 | tf_op jit(solution)/shard_map/ppermute | solution.py:48
  93.7 1.3 copy-done.1
  95.0 1.3 mix.1
  96.3 1.4 collective-permute-start.13
  97.8 0.9 collective-permute-start.12
  99.3 4.1 %all-to-all-start.1 = ((f32[8,16,128]{2,1,0:T(8,128)}), f32[8,16,128]{2,1,0:T(8,128)S(1)}, u32[]{:S(2)}, u32[]{:S(2)}) async-start(f32[8,16,128]{2,1,0:T(8,128)} %get-tuple-element.60), calls=%async_computation.1 | async-start | bytes 131072 | tf_op jit(solution)/shard_map/all_to_all | solution.py:522
  103.5 12.5 %all-to-all-done.1 = f32[8,16,128]{2,1,0:T(8,128)S(1)} async-done(((f32[8,16,128]{2,1,0:T(8,128)}), f32[8,16,128]{2,1,0:T(8,128)S(1)}, u32[]{:S(2)}, u32[]{:S(2)}) %all-to-all-start.1) | async-done | bytes 65568 | tf_op jit(solution)/shard_map/all_to_all | solution.py:522
  116.0 1.3 slice.45
  117.4 1.3 pad_maximum_fusion
  118.7 0.9 collective-permute-start.16
  119.9 1.2 collective-permute-start.14
  121.8 5.3 %norm.2 = (bf16[2048,640]{1,0:T(8,128)(2,1)}, bf16[4,64,640]{2,1,0:T(8,128)(2,1)}) custom-call(s32[10]{0:T(128)} %stack.43.where_ref, f32[8,512]{1,0:T(8,128)} %maximum_maximum_fusion.norm_ref.refs_12_, f32[8,2,640]{2,1,0:T(2,128)} %bitcast.48, bf16[512,640]{1,0:T(8,128)(2,1)} %copy-done.2, bf16[512,640]{1,0:T(8,128)(2,1)} %collective-permute-done.11.refs_1_, ...), custom_call_target="tpu_custom_call" | custom-call | flops 1 | bytes 1 | tf_op jit(solution)/shard_map/norm/pallas_call | solution.py:225
  127.2 2.8 %collective-permute-start.21 = (bf16[2048,640]{1,0:T(8,128)(2,1)}, bf16[2048,640]{1,0:T(8,128)(2,1)}, u32[]{:S(2)}, u32[]{:S(2)}) collective-permute-start(bf16[2048,640]{1,0:T(8,128)(2,1)} %get-tuple-element.65.refs_0_), channel_id=1, source_target_pairs={{0,128},{128,0},{1,129},{129,1},{2,130},{130,2},{3,131},{131,3},{4... | collective-permute-start | bytes 7864328 | tf_op jit(solution)/shard_map/ppermute | solution.py:48
  130.0 3.5 %collective-permute-done.16.refs_2_ = bf16[512,640]{1,0:T(8,128)(2,1)S(1)} collective-permute-done((bf16[512,640]{1,0:T(8,128)(2,1)}, bf16[512,640]{1,0:T(8,128)(2,1)S(1)}, u32[]{:S(2)}, u32[]{:S(2)}) %collective-permute-start.16) | collective-permute-done | bytes 655392 | tf_op jit(solution)/shard_map/ppermute | solution.py:40
  134.0 1.4 collective-permute-done.14.refs_0_
  135.5 3.1 %collective-permute-start.20 = (f32[8,512]{1,0:T(8,128)S(1)}, f32[8,512]{1,0:T(8,128)S(1)}, u32[]{:S(2)}, u32[]{:S(2)}) collective-permute-start(f32[8,512]{1,0:T(8,128)S(1)} %copy-done.20), channel_id=1, source_target_pairs={{0,128},{128,0},{1,129},{129,1},{2,130},{130,2},{3,131},{131,3},{4... | collective-permute-start | bytes 49160 | tf_op jit(solution)/shard_map/ppermute | solution.py:48
  139.9 2.6 %collective-permute-start.19 = (bf16[192,640]{1,0:T(8,128)(2,1)S(1)}, bf16[192,640]{1,0:T(8,128)(2,1)S(1)}, u32[]{:S(2)}, u32[]{:S(2)}) collective-permute-start(bf16[192,640]{1,0:T(8,128)(2,1)S(1)} %slice.52), channel_id=1, source_target_pairs={{0,96},{16,112},{32,0},{48,16},{64,32},{80,48},{96,64},{112,80},{1... | collective-permute-start | bytes 737288 | tf_op jit(solution)/shard_map/ppermute | solution.py:40
  142.5 3.5 %sine_multiply_fusion = (f32[1024,128]{1,0:T(8,128)}, f32[1024,128]{1,0:T(8,128)}) fusion(f32[128]{0:T(128)S(1)} %get-tuple-element.102, f32[128]{0:T(128)S(1)} %get-tuple-element.103, s32[1024]{0:T(1024)S(1)} %get-tuple-element.101, s32[1024]{0:T(1024)S(1)} %get-tuple-element.100, s32[1024]{0:T(1024)S(1)} %get-tuple-element.99, ...), kind=kLoop, calls=%fused_computation.7 | loop fusion | flops 655360 | bytes 1062144 | tf_op jit(solution)/shard_map/mul | solution.py:461
  146.0 4.5 %norm.3 = (bf16[1536,640]{1,0:T(8,128)(2,1)}, bf16[3,64,640]{2,1,0:T(8,128)(2,1)}) custom-call(s32[10]{0:T(128)} %stack.43.where_ref, f32[8,512]{1,0:T(8,128)} %maximum_maximum_fusion.norm_ref.refs_12_, f32[8,2,640]{2,1,0:T(2,128)} %bitcast.49, bf16[512,640]{1,0:T(8,128)(2,1)} %copy-done.14, bf16[512,640]{1,0:T(8,128)(2,1)} %copy-done.18, ...), custom_call_target="tpu_custom_call" | custom-call | flops 1 | bytes 1 | tf_op jit(solution)/shard_map/norm/pallas_call | solution.py:225
  150.6 1.0 collective-permute-start.22
  152.2 0.9 copy-done.6
  154.0 1.7 collective-permute-done.24.refs_8_
  156.7 13.9 %project.1 = (f32[1024,640]{1,0:T(8,128)}, f32[8,8,128]{2,1,0:T(8,128)}) custom-call(s32[10]{0:T(128)} %stack.43.where_ref, bf16[2048,640]{1,0:T(8,128)(2,1)} %get-tuple-element.65.refs_0_, bf16[1536,640]{1,0:T(8,128)(2,1)} %get-tuple-element.72.refs_1_, bf16[192,640]{1,0:T(8,128)(2,1)} %copy-done.4, bf16[128,640]{1,0:T(8,128)(2,1)} %copy-done.7, ...), custom_call_target="tpu_custom_call" | custom-call | flops 6710886400 | bytes 19660800 | tf_op jit(solution)/shard_map/project/pallas_call | solution.py:374
  170.6 3.3 %all-to-all-start.2 = ((f32[8,8,128]{2,1,0:T(8,128)}), f32[8,8,128]{2,1,0:T(8,128)S(1)}, u32[]{:S(2)}, u32[]{:S(2)}) async-start(f32[8,8,128]{2,1,0:T(8,128)} %get-tuple-element.81), calls=%async_computation.2 | async-start | bytes 65536 | tf_op jit(solution)/shard_map/all_to_all | solution.py:571
  174.0 0.9 maximum_select_fusion.1
  174.9 5.4 %turn.1 = f32[1024,640]{1,0:T(8,128)} custom-call(s32[10]{0:T(128)} %stack.43.where_ref, f32[1024,640]{1,0:T(8,128)} %get-tuple-element.82.proj_ref, f32[1,640]{1,0:T(1,128)} %gain_ref.1, f32[1024,128]{1,0:T(8,128)} %get-tuple-element.83.cos_ref, f32[1024,128]{1,0:T(8,128)} %get-tuple-element.84.sin_ref), custom_call_target="tpu_custom_call" | custom-call | flops 6553600 | bytes 5898240 | tf_op jit(solution)/shard_map/turn/pallas_call | solution.py:425
  180.5 3.0 %fusion = bf16[1,1,1024,640]{3,2,1,0:T(8,128)(2,1)} fusion(f32[1024,640]{1,0:T(8,128)} %turn.1, f32[1024]{0:T(1024)S(1)} %mul.75), kind=kLoop, calls=%fused_computation.1 | loop fusion | flops 1310720 | bytes 3936256 | tf_op jit(solution)/shard_map/broadcast_in_dim | solution.py:584
  (115 shorter events, 9.7 us)
Async XLA Ops:
  7.2 49.0 %copy-start = (bf16[1,128,5120]{2,1,0:T(8,128)(2,1)S(1)}, bf16[1,128,5120]{2,1,0:T(8,128)(2,1)}, u32[]{:S(2)}) copy-start(bf16[1,128,5120]{2,1,0:T(8,128)(2,1)} %param.10) | copy-start | bytes 3932164
  7.2 34.6 %copy-start.19 = (bf16[1,320,640]{2,1,0:T(8,128)(2,1)S(1)}, bf16[1,320,640]{2,1,0:T(8,128)(2,1)}, u32[]{:S(2)}) copy-start(bf16[1,320,640]{2,1,0:T(8,128)(2,1)} %param.15) | copy-start | bytes 1228804
  7.2 66.8 %all-gather.4.cloned.1.call-start = ((), (), s32[]{:S(2)}) async-start(), calls=%async_computation.3 | async-start | bytes 3686400 | tf_op jit(solution)/shard_map/all_gather | solution.py:494
  7.2 7.7 %collective-permute-start = (bf16[160,640]{1,0:T(8,128)(2,1)}, bf16[160,640]{1,0:T(8,128)(2,1)S(1)}, u32[]{:S(2)}, u32[]{:S(2)}) collective-permute-start(bf16[160,640]{1,0:T(8,128)(2,1)} %param.13), channel_id=1, source_target_pairs={{0,8},{1,9},{2,10},{3,11},{4,12},{5,13},{6,14},{7,15},{8,0},{9,1},... | collective-permute-start | bytes 614408 | tf_op jit(solution)/shard_map/ppermute | solution.py:44
  16.9 137.1 %all-gather.6.cloned.1.call-start = ((), (), s32[]{:S(2)}) async-start(), calls=%async_computation.4 | async-start | bytes 7372800 | tf_op jit(solution)/shard_map/all_gather | solution.py:494
  16.9 16.5 %collective-permute-start.2 = (bf16[128,2560]{1,0:T(8,128)(2,1)}, bf16[128,2560]{1,0:T(8,128)(2,1)S(1)}, u32[]{:S(2)}, u32[]{:S(2)}) collective-permute-start(bf16[128,2560]{1,0:T(8,128)(2,1)} %bitcast.39), channel_id=1, source_target_pairs={{0,96},{16,112},{32,0},{48,16},{64,32},{80,48},{96,64},{112,80},{1... | collective-permute-start | bytes 1966088 | tf_op jit(solution)/shard_map/ppermute | solution.py:40
  20.6 15.8 %collective-permute-start.1 = (bf16[128,2560]{1,0:T(8,128)(2,1)}, bf16[128,2560]{1,0:T(8,128)(2,1)S(1)}, u32[]{:S(2)}, u32[]{:S(2)}) collective-permute-start(bf16[128,2560]{1,0:T(8,128)(2,1)} %bitcast.40), channel_id=1, source_target_pairs={{0,32},{16,48},{32,64},{48,80},{64,96},{80,112},{96,0},{112,16},{1... | collective-permute-start | bytes 1966088 | tf_op jit(solution)/shard_map/ppermute | solution.py:40
  20.6 10.8 %collective-permute-start.3 = (bf16[320,640]{1,0:T(8,128)(2,1)}, bf16[320,640]{1,0:T(8,128)(2,1)S(1)}, u32[]{:S(2)}, u32[]{:S(2)}) collective-permute-start(bf16[320,640]{1,0:T(8,128)(2,1)} %bitcast.44), channel_id=1, source_target_pairs={{0,8},{1,9},{2,10},{3,11},{4,12},{5,13},{6,14},{7,15},{8,0},{9,1},... | collective-permute-start | bytes 1228808 | tf_op jit(solution)/shard_map/ppermute | solution.py:44
  33.4 9.7 %copy-start.11 = (bf16[128,2560]{1,0:T(8,128)(2,1)}, bf16[128,2560]{1,0:T(8,128)(2,1)S(1)}, u32[]{:S(2)}) copy-start(bf16[128,2560]{1,0:T(8,128)(2,1)S(1)} %collective-permute-done.2.refs_2_) | copy-start | bytes 1966084
  36.4 6.6 %copy-start.12 = (bf16[128,2560]{1,0:T(8,128)(2,1)}, bf16[128,2560]{1,0:T(8,128)(2,1)S(1)}, u32[]{:S(2)}) copy-start(bf16[128,2560]{1,0:T(8,128)(2,1)S(1)} %collective-permute-done.1.refs_1_) | copy-start | bytes 1966084
  36.4 13.8 %collective-permute-start.6 = (bf16[128,2560]{1,0:T(8,128)(2,1)}, bf16[128,2560]{1,0:T(8,128)(2,1)}, u32[]{:S(2)}, u32[]{:S(2)}) collective-permute-start(bf16[128,2560]{1,0:T(8,128)(2,1)} %bitcast.41), channel_id=1, source_target_pairs={{0,16},{16,0},{32,48},{48,32},{64,80},{80,64},{96,112},{112,96},{1... | collective-permute-start | bytes 1966088 | tf_op jit(solution)/shard_map/ppermute | solution.py:40
  39.1 7.7 %collective-permute-start.4 = (bf16[64,2560]{1,0:T(8,128)(2,1)}, bf16[64,2560]{1,0:T(8,128)(2,1)}, u32[]{:S(2)}, u32[]{:S(2)}) collective-permute-start(bf16[64,2560]{1,0:T(8,128)(2,1)} %slice.41), channel_id=1, source_target_pairs={{0,32},{16,48},{32,64},{48,80},{64,96},{80,112},{96,0},{112,16},{1... | collective-permute-start | bytes 983048 | tf_op jit(solution)/shard_map/ppermute | solution.py:40
  39.1 7.7 %collective-permute-start.5 = (bf16[64,2560]{1,0:T(8,128)(2,1)}, bf16[64,2560]{1,0:T(8,128)(2,1)}, u32[]{:S(2)}, u32[]{:S(2)}) collective-permute-start(bf16[64,2560]{1,0:T(8,128)(2,1)} %slice.42), channel_id=1, source_target_pairs={{0,96},{16,112},{32,0},{48,16},{64,32},{80,48},{96,64},{112,80},{1... | collective-permute-start | bytes 983048 | tf_op jit(solution)/shard_map/ppermute | solution.py:40
  50.2 23.7 %collective-permute-start.8 = (bf16[128,2560]{1,0:T(8,128)(2,1)}, bf16[128,2560]{1,0:T(8,128)(2,1)S(1)}, u32[]{:S(2)}, u32[]{:S(2)}) collective-permute-start(bf16[128,2560]{1,0:T(8,128)(2,1)} %collective-permute-done.6.refs_3_), channel_id=1, source_target_pairs={{0,32},{16,48},{32,64},{48,80},{64,96},{80,112},{96,0},{112,16},{1... | collective-permute-start | bytes 1966088 | tf_op jit(solution)/shard_map/ppermute | solution.py:40
  50.3 23.6 %collective-permute-start.7 = (bf16[128,2560]{1,0:T(8,128)(2,1)}, bf16[128,2560]{1,0:T(8,128)(2,1)S(1)}, u32[]{:S(2)}, u32[]{:S(2)}) collective-permute-start(bf16[128,2560]{1,0:T(8,128)(2,1)} %collective-permute-done.6.refs_3_), channel_id=1, source_target_pairs={{0,96},{16,112},{32,0},{48,16},{64,32},{80,48},{96,64},{112,80},{1... | collective-permute-start | bytes 1966088 | tf_op jit(solution)/shard_map/ppermute | solution.py:40
  55.0 18.9 %collective-permute-start.9 = (bf16[128,2560]{1,0:T(8,128)(2,1)}, bf16[128,2560]{1,0:T(8,128)(2,1)}, u32[]{:S(2)}, u32[]{:S(2)}) collective-permute-start(bf16[128,2560]{1,0:T(8,128)(2,1)} %join.1.refs_4_), channel_id=1, source_target_pairs={{0,16},{16,0},{32,48},{48,32},{64,80},{80,64},{96,112},{112,96},{1... | collective-permute-start | bytes 1966088 | tf_op jit(solution)/shard_map/ppermute | solution.py:40
  57.2 16.7 %all-to-all-start = ((bf16[8,64,640]{2,1,0:T(8,128)(2,1)}), bf16[8,64,640]{2,1,0:T(8,128)(2,1)S(1)}, u32[]{:S(2)}, u32[]{:S(2)}) async-start(bf16[8,64,640]{2,1,0:T(8,128)(2,1)} %copy.14), calls=%async_computation | async-start | bytes 1310720 | tf_op jit(solution)/shard_map/all_to_all | solution.py:504
  73.9 16.9 %copy-start.21 = (f32[640]{0:T(1024)S(1)}, f32[640]{0:T(1024)}, u32[]{:S(2)}) copy-start(f32[640]{0:T(1024)} %param.14) | copy-start | bytes 7684
  73.9 19.7 %copy-start.9 = (s32[1,128]{1,0:T(1,128)S(1)}, s32[1,128]{1,0:T(1,128)}, u32[]{:S(2)}) copy-start(s32[1,128]{1,0:T(1,128)} %cell_ref.1) | copy-start | bytes 1540
  85.3 8.3 %collective-permute-start.10 = (f32[512,640]{1,0:T(8,128)}, f32[512,640]{1,0:T(8,128)S(1)}, u32[]{:S(2)}, u32[]{:S(2)}) collective-permute-start(f32[512,640]{1,0:T(8,128)} %get-tuple-element.57), channel_id=1, source_target_pairs={{0,128},{128,0},{1,129},{129,1},{2,130},{130,2},{3,131},{131,3},{4... | collective-permute-start | bytes 3932168 | tf_op jit(solution)/shard_map/ppermute | solution.py:48
  96.3 21.0 %copy-start.2 = (bf16[512,640]{1,0:T(8,128)(2,1)}, bf16[512,640]{1,0:T(8,128)(2,1)S(1)}, u32[]{:S(2)}) copy-start(bf16[512,640]{1,0:T(8,128)(2,1)S(1)} %get-tuple-element.59.refs_0_) | copy-start | bytes 1966084
  96.3 19.6 %collective-permute-start.13 = (bf16[512,640]{1,0:T(8,128)(2,1)S(1)}, bf16[512,640]{1,0:T(8,128)(2,1)S(1)}, u32[]{:S(2)}, u32[]{:S(2)}) collective-permute-start(bf16[512,640]{1,0:T(8,128)(2,1)S(1)} %get-tuple-element.59.refs_0_), channel_id=1, source_target_pairs={{0,16},{16,0},{32,48},{48,32},{64,80},{80,64},{96,112},{112,96},{1... | collective-permute-start | bytes 1966088 | tf_op jit(solution)/shard_map/ppermute | solution.py:40
  97.8 18.2 %collective-permute-start.12 = (bf16[512,640]{1,0:T(8,128)(2,1)S(1)}, bf16[512,640]{1,0:T(8,128)(2,1)S(1)}, u32[]{:S(2)}, u32[]{:S(2)}) collective-permute-start(bf16[512,640]{1,0:T(8,128)(2,1)S(1)} %get-tuple-element.59.refs_0_), channel_id=1, source_target_pairs={{0,96},{16,112},{32,0},{48,16},{64,32},{80,48},{96,64},{112,80},{1... | collective-permute-start | bytes 1966088 | tf_op jit(solution)/shard_map/ppermute | solution.py:40
  98.7 17.3 %collective-permute-start.11 = (bf16[512,640]{1,0:T(8,128)(2,1)S(1)}, bf16[512,640]{1,0:T(8,128)(2,1)}, u32[]{:S(2)}, u32[]{:S(2)}) collective-permute-start(bf16[512,640]{1,0:T(8,128)(2,1)S(1)} %get-tuple-element.59.refs_0_), channel_id=1, source_target_pairs={{0,32},{16,48},{32,64},{48,80},{64,96},{80,112},{96,0},{112,16},{1... | collective-permute-start | bytes 1966088 | tf_op jit(solution)/shard_map/ppermute | solution.py:40
  99.3 16.6 %all-to-all-start.1 = ((f32[8,16,128]{2,1,0:T(8,128)}), f32[8,16,128]{2,1,0:T(8,128)S(1)}, u32[]{:S(2)}, u32[]{:S(2)}) async-start(f32[8,16,128]{2,1,0:T(8,128)} %get-tuple-element.60), calls=%async_computation.1 | async-start | bytes 131072 | tf_op jit(solution)/shard_map/all_to_all | solution.py:522
  118.7 14.7 %collective-permute-start.16 = (bf16[512,640]{1,0:T(8,128)(2,1)}, bf16[512,640]{1,0:T(8,128)(2,1)S(1)}, u32[]{:S(2)}, u32[]{:S(2)}) collective-permute-start(bf16[512,640]{1,0:T(8,128)(2,1)} %get-tuple-element.94), channel_id=1, source_target_pairs={{0,16},{16,0},{32,48},{48,32},{64,80},{80,64},{96,112},{112,96},{1... | collective-permute-start | bytes 1966088 | tf_op jit(solution)/shard_map/ppermute | solution.py:40
  119.6 14.3 %collective-permute-start.15 = (bf16[512,640]{1,0:T(8,128)(2,1)}, bf16[512,640]{1,0:T(8,128)(2,1)S(1)}, u32[]{:S(2)}, u32[]{:S(2)}) collective-permute-start(bf16[512,640]{1,0:T(8,128)(2,1)} %get-tuple-element.95), channel_id=1, source_target_pairs={{0,96},{16,112},{32,0},{48,16},{64,32},{80,48},{96,64},{112,80},{1... | collective-permute-start | bytes 1966088 | tf_op jit(solution)/shard_map/ppermute | solution.py:40
  119.9 15.5 %collective-permute-start.14 = (bf16[512,640]{1,0:T(8,128)(2,1)}, bf16[512,640]{1,0:T(8,128)(2,1)S(1)}, u32[]{:S(2)}, u32[]{:S(2)}) collective-permute-start(bf16[512,640]{1,0:T(8,128)(2,1)} %get-tuple-element.96), channel_id=1, source_target_pairs={{0,32},{16,48},{32,64},{48,80},{64,96},{80,112},{96,0},{112,16},{1... | collective-permute-start | bytes 1966088 | tf_op jit(solution)/shard_map/ppermute | solution.py:40
  127.2 8.3 %copy-start.20 = (f32[8,512]{1,0:T(8,128)S(1)}, f32[8,512]{1,0:T(8,128)}, u32[]{:S(2)}) copy-start(f32[8,512]{1,0:T(8,128)} %maximum_maximum_fusion.norm_ref.refs_12_) | copy-start | bytes 49156
  127.2 28.9 %collective-permute-start.21 = (bf16[2048,640]{1,0:T(8,128)(2,1)}, bf16[2048,640]{1,0:T(8,128)(2,1)}, u32[]{:S(2)}, u32[]{:S(2)}) collective-permute-start(bf16[2048,640]{1,0:T(8,128)(2,1)} %get-tuple-element.65.refs_0_), channel_id=1, source_target_pairs={{0,128},{128,0},{1,129},{129,1},{2,130},{130,2},{3,131},{131,3},{4... | collective-permute-start | bytes 7864328 | tf_op jit(solution)/shard_map/ppermute | solution.py:48
  133.5 12.6 %copy-start.13 = (bf16[512,640]{1,0:T(8,128)(2,1)}, bf16[512,640]{1,0:T(8,128)(2,1)S(1)}, u32[]{:S(2)}) copy-start(bf16[512,640]{1,0:T(8,128)(2,1)S(1)} %collective-permute-done.16.refs_2_) | copy-start | bytes 1966084
  134.0 4.7 %copy-start.18 = (bf16[512,640]{1,0:T(8,128)(2,1)}, bf16[512,640]{1,0:T(8,128)(2,1)S(1)}, u32[]{:S(2)}) copy-start(bf16[512,640]{1,0:T(8,128)(2,1)S(1)} %collective-permute-done.15.refs_1_) | copy-start | bytes 1966084
  135.4 3.9 %copy-start.14 = (bf16[512,640]{1,0:T(8,128)(2,1)}, bf16[512,640]{1,0:T(8,128)(2,1)S(1)}, u32[]{:S(2)}) copy-start(bf16[512,640]{1,0:T(8,128)(2,1)S(1)} %collective-permute-done.14.refs_0_) | copy-start | bytes 1966084
  135.5 15.1 %collective-permute-start.20 = (f32[8,512]{1,0:T(8,128)S(1)}, f32[8,512]{1,0:T(8,128)S(1)}, u32[]{:S(2)}, u32[]{:S(2)}) collective-permute-start(f32[8,512]{1,0:T(8,128)S(1)} %copy-done.20), channel_id=1, source_target_pairs={{0,128},{128,0},{1,129},{129,1},{2,130},{130,2},{3,131},{131,3},{4... | collective-permute-start | bytes 49160 | tf_op jit(solution)/shard_map/ppermute | solution.py:48
  139.3 11.2 %collective-permute-start.18 = (bf16[128,640]{1,0:T(8,128)(2,1)}, bf16[128,640]{1,0:T(8,128)(2,1)S(1)}, u32[]{:S(2)}, u32[]{:S(2)}) collective-permute-start(bf16[128,640]{1,0:T(8,128)(2,1)} %pad_maximum_fusion.3), channel_id=1, source_target_pairs={{0,32},{16,48},{32,64},{48,80},{64,96},{80,112},{96,0},{112,16},{1... | collective-permute-start | bytes 491528 | tf_op jit(solution)/shard_map/ppermute | solution.py:40
  139.3 11.2 %collective-permute-start.17 = (bf16[192,640]{1,0:T(8,128)(2,1)S(1)}, bf16[192,640]{1,0:T(8,128)(2,1)S(1)}, u32[]{:S(2)}, u32[]{:S(2)}) collective-permute-start(bf16[192,640]{1,0:T(8,128)(2,1)S(1)} %slice.49), channel_id=1, source_target_pairs={{0,16},{16,0},{32,48},{48,32},{64,80},{80,64},{96,112},{112,96},{1... | collective-permute-start | bytes 737288 | tf_op jit(solution)/shard_map/ppermute | solution.py:40
  139.9 10.7 %collective-permute-start.19 = (bf16[192,640]{1,0:T(8,128)(2,1)S(1)}, bf16[192,640]{1,0:T(8,128)(2,1)S(1)}, u32[]{:S(2)}, u32[]{:S(2)}) collective-permute-start(bf16[192,640]{1,0:T(8,128)(2,1)S(1)} %slice.52), channel_id=1, source_target_pairs={{0,96},{16,112},{32,0},{48,16},{64,32},{80,48},{96,64},{112,80},{1... | collective-permute-start | bytes 737288 | tf_op jit(solution)/shard_map/ppermute | solution.py:40
  142.5 9.7 %copy-start.3 = (bf16[4,64,640]{2,1,0:T(8,128)(2,1)S(1)}, bf16[4,64,640]{2,1,0:T(8,128)(2,1)}, u32[]{:S(2)}) copy-start(bf16[4,64,640]{2,1,0:T(8,128)(2,1)} %get-tuple-element.77.first_ref) | copy-start | bytes 983044
  142.5 9.7 %copy-start.8 = (s32[10]{0:T(128)S(1)}, s32[10]{0:T(128)}, u32[]{:S(2)}) copy-start(s32[10]{0:T(128)} %stack.43.where_ref) | copy-start | bytes 124
  150.6 3.3 %copy-start.24 = (f32[8,512]{1,0:T(8,128)}, f32[8,512]{1,0:T(8,128)S(1)}, u32[]{:S(2)}) copy-start(f32[8,512]{1,0:T(8,128)S(1)} %collective-permute-done.20.refs_13_) | copy-start | bytes 49156
  150.6 3.3 %copy-start.7 = (bf16[128,640]{1,0:T(8,128)(2,1)}, bf16[128,640]{1,0:T(8,128)(2,1)S(1)}, u32[]{:S(2)}) copy-start(bf16[128,640]{1,0:T(8,128)(2,1)S(1)} %collective-permute-done.18.refs_1_.refs_3_) | copy-start | bytes 491524
  150.6 3.3 %copy-start.4 = (bf16[192,640]{1,0:T(8,128)(2,1)}, bf16[192,640]{1,0:T(8,128)(2,1)S(1)}, u32[]{:S(2)}) copy-start(bf16[192,640]{1,0:T(8,128)(2,1)S(1)} %collective-permute-done.17.refs_0_.refs_2_) | copy-start | bytes 737284
  150.6 5.8 %collective-permute-start.22 = (bf16[1536,640]{1,0:T(8,128)(2,1)}, bf16[1536,640]{1,0:T(8,128)(2,1)}, u32[]{:S(2)}, u32[]{:S(2)}) collective-permute-start(bf16[1536,640]{1,0:T(8,128)(2,1)} %get-tuple-element.72.refs_1_), channel_id=1, source_target_pairs={{0,128},{128,0},{1,129},{129,1},{2,130},{130,2},{3,131},{131,3},{4... | collective-permute-start | bytes 5898248 | tf_op jit(solution)/shard_map/ppermute | solution.py:48
  151.6 4.1 %collective-permute-start.24 = (bf16[128,640]{1,0:T(8,128)(2,1)S(1)}, bf16[128,640]{1,0:T(8,128)(2,1)}, u32[]{:S(2)}, u32[]{:S(2)}) collective-permute-start(bf16[128,640]{1,0:T(8,128)(2,1)S(1)} %collective-permute-done.18.refs_1_.refs_3_), channel_id=1, source_target_pairs={{0,128},{128,0},{1,129},{129,1},{2,130},{130,2},{3,131},{131,3},{4... | collective-permute-start | bytes 491528 | tf_op jit(solution)/shard_map/ppermute | solution.py:48
  151.7 4.1 %collective-permute-start.23 = (bf16[192,640]{1,0:T(8,128)(2,1)S(1)}, bf16[192,640]{1,0:T(8,128)(2,1)S(1)}, u32[]{:S(2)}, u32[]{:S(2)}) collective-permute-start(bf16[192,640]{1,0:T(8,128)(2,1)S(1)} %collective-permute-done.17.refs_0_.refs_2_), channel_id=1, source_target_pairs={{0,128},{128,0},{1,129},{129,1},{2,130},{130,2},{3,131},{131,3},{4... | collective-permute-start | bytes 737288 | tf_op jit(solution)/shard_map/ppermute | solution.py:48
  152.1 3.9 %collective-permute-start.25 = (bf16[192,640]{1,0:T(8,128)(2,1)S(1)}, bf16[192,640]{1,0:T(8,128)(2,1)S(1)}, u32[]{:S(2)}, u32[]{:S(2)}) collective-permute-start(bf16[192,640]{1,0:T(8,128)(2,1)S(1)} %collective-permute-done.19.refs_2_.refs_4_), channel_id=1, source_target_pairs={{0,128},{128,0},{1,129},{129,1},{2,130},{130,2},{3,131},{131,3},{4... | collective-permute-start | bytes 737288 | tf_op jit(solution)/shard_map/ppermute | solution.py:48
  155.7 18.3 %collective-permute-start.26 = (bf16[64,2560]{1,0:T(8,128)(2,1)S(1)}, bf16[64,2560]{1,0:T(8,128)(2,1)S(1)}, u32[]{:S(2)}, u32[]{:S(2)}) collective-permute-start(bf16[64,2560]{1,0:T(8,128)(2,1)S(1)} %get-tuple-element.91), channel_id=1, source_target_pairs={{0,128},{128,0},{1,129},{129,1},{2,130},{130,2},{3,131},{131,3},{4... | collective-permute-start | bytes 983048 | tf_op jit(solution)/shard_map/ppermute | solution.py:48
  170.6 9.7 %all-to-all-start.2 = ((f32[8,8,128]{2,1,0:T(8,128)}), f32[8,8,128]{2,1,0:T(8,128)S(1)}, u32[]{:S(2)}, u32[]{:S(2)}) async-start(f32[8,8,128]{2,1,0:T(8,128)} %get-tuple-element.81), calls=%async_computation.2 | async-start | bytes 65536 | tf_op jit(solution)/shard_map/all_to_all | solution.py:571
  (9 other events, 11.6 us)
Sparse Core Ops, SparseCore 0:
  17.0 50.9 all-gather.3
  69.7 75.5 all-gather.5

commit v2 on v1

--- a/solution.py
+++ b/solution.py
@@ -61,41 +61,35 @@
     return jnp.concatenate(parts, 0)
 
 
-def join_kernel(a_ref, b_ref, out_ref):
-    half = a_ref.shape[0]
-    out_ref[:half, :] = a_ref[...]
-    out_ref[half:, :] = b_ref[...]
-
-
-def join(a, b):
-    return pl.pallas_call(
-        join_kernel,
-        out_shape=jax.ShapeDtypeStruct((2 * a.shape[0], a.shape[1]), a.dtype),
-        in_specs=[WHOLE] * 2,
+def split_kernel(where_ref, main_ref, out_ref):
+    tokens, width = out_ref.shape[1:]
+    at = pl.ds(pl.multiple_of(where_ref[8] * tokens, 16), tokens)
+    for s in range(NS):
+        out_ref[s] = main_ref[at, s * width : (s + 1) * width]
+
+
+def split_columns(where, main):
+    tokens, features = main.shape
+    return pl.pallas_call(
+        split_kernel,
+        out_shape=jax.ShapeDtypeStruct((NS, tokens // 2, features // NS), main.dtype),
+        in_specs=[SCALARS, WHOLE],
         out_specs=WHOLE,
+        compiler_params=pltpu.CompilerParams(vmem_limit_bytes=16 * MIB),
         cost_estimate=SMALL,
-        name="join",
-    )(a, b)
-
-
-def relay_context(own, beside_first, beside_second, beside_third):
-    half = own.shape[0] // 2
-    back, ahead, extra = lax.optimization_barrier(
-        (seq_send(own, 1, 0), seq_send(own, -1, 0), beside_first)
-    )
-    up, down, beside, more = lax.optimization_barrier(
-        (
-            seq_send(back[:half], 1, 0),
-            seq_send(ahead[half:], -1, 0),
-            seq_send(after(own, back), 0, 1),
-            beside_second(extra),
-        )
-    )
-    far = join(up, down)
-    ahead_beside, back_beside, far_beside, extra = lax.optimization_barrier(
-        (seq_send(beside, -1, 0), seq_send(beside, 1, 0), seq_send(far, 0, 1), beside_third(beside))
-    )
-    return [own, back, ahead, beside, far, ahead_beside, back_beside, far_beside], more, extra
+        name="split_columns",
+    )(where, main)
+
+
+def relay_context(own, slot_other, join_slot, main_half, where):
+    back, ahead, slot_other = lax.optimization_barrier((seq_send(own, 1, 0), seq_send(own, -1, 0), slot_other))
+    far, beside, slot_both = lax.optimization_barrier(
+        (seq_send(back, 1, 0), seq_send(after(own, back), 0, 1), join_slot(slot_other))
+    )
+    ahead_beside, back_beside, far_beside, main_half, where = lax.optimization_barrier(
+        (seq_send(beside, -1, 0), seq_send(beside, 1, 0), seq_send(far, 0, 1), main_half, where)
+    )
+    return [own, back, ahead, beside, far, ahead_beside, back_beside, far_beside], slot_both, main_half, where
 
 
 def hint_kernel(rows, where_ref, weight_ref, *refs):
@@ -103,7 +97,7 @@
     other_ref, mine_ref, ctx, wgt, sem = refs[NS:]
     half_rows = rows // 2
     depth = weight_ref.shape[1] // NH
-    mine = where_ref[8]
+    mine, column = where_ref[8], where_ref[10]
     copies = []
 
     def copy(src, dst):
@@ -116,17 +110,28 @@
             src = pl.ds(pl.multiple_of(half * half_rows, 16), half_rows)
             copy(block.at[src], ctx.at[slot, pl.ds(pl.multiple_of(where_ref[i] * half_rows, 16), half_rows)])
 
+    def column_rows(col):
+        first = jnp.where(col == column, 0, depth)
+        for z in range(NZ):
+            src = pl.ds(pl.multiple_of(first, 16), depth)
+            copy(weight_ref.at[z, src], wgt.at[pl.ds((col * NZ + z) * depth, depth)])
+
     tokens(1 - mine, 0)
-    for h in range(NH):
-        for z in range(NZ):
-            copy(weight_ref.at[z, pl.ds(h * depth, depth)], wgt.at[pl.ds((h * NZ + z) * depth, depth)])
+    column_rows(0)
+    column_rows(1)
     tokens(mine, 1)
-    for c in copies[: NS + NH * NZ]:
-        c.wait()
-    other_ref[...] = jnp.dot(ctx[0], wgt[...], preferred_element_type=F32)
-    for c in copies[NS + NH * NZ :]:
-        c.wait()
-    mine_ref[...] = jnp.dot(ctx[1], wgt[...], preferred_element_type=F32)
+    deep = NZ * depth
+    done = 0
+    for count, out_ref, slot, k in ((NS + NZ, other_ref, 0, 0), (NZ, other_ref, 0, 1), (NS, mine_ref, 1, None)):
+        for c in copies[done : done + count]:
+            c.wait()
+        done += count
+        if k is None:
+            out_ref[...] = jnp.dot(ctx[slot], wgt[...], preferred_element_type=F32)
+        else:
+            lanes = slice(k * deep, (k + 1) * deep)
+            product = jnp.dot(ctx[slot, :, lanes], wgt[lanes, :], preferred_element_type=F32)
+            out_ref[...] = out_ref[...] + product if k else product
 
 
 def hint_matmul(where, blocks, weight):
@@ -330,6 +335,7 @@
         rstd[at, :] = jnp.broadcast_to(ref[1:2, :], (128, rows)).T
     s = where_ref[NS - 1]
     shift, scale = mod_ref[s, 0:1, :], 1.0 + mod_ref[s, 1:2, :]
+    sums = []
     for i in range(0, NS, 2):
         for c in copies[i] + copies[i + 1]:
             c.wait()
@@ -350,13 +356,13 @@
             product = jnp.dot(xs[at, deep_lanes], wgt[deep_lanes, :], preferred_element_type=F32)
             if i == 0:
                 out_ref[at, :] = product + bias_ref[...]
+            elif i < NS - 2:
+                out_ref[at, :] += product
             else:
-                out_ref[at, :] += product
+                values = out_ref[at, :] + product
+                out_ref[at, :] = values
+                sums.append(jnp.sum(values * values, axis=-1, keepdims=True))
     lane = lax.broadcasted_iota(jnp.int32, (rows, 128), 1)
-    sums = []
-    for part in range(2):
-        values = out_ref[pl.ds(part * rows, rows), :]
-        sums.append(jnp.sum(values * values, axis=-1, keepdims=True))
     both = jnp.where(lane == 0, sums[0], sums[1]).T
     lines = rows // 128
     for d in range(NS):
@@ -478,7 +484,7 @@
     y, x = seq // NX, seq % NX
     hh = dp // NZ
     where = jnp.stack(
-        [((y + dy) % NY) * NX + (x + dx) % NX for dy, dx in REL] + [branch, seq]
+        [((y + dy) % NY) * NX + (x + dx) % NX for dy, dx in REL] + [branch, seq, hh]
     ).astype(jnp.int32)
 
     tokens, features = main_stream.shape[1:]
@@ -487,32 +493,26 @@
     rows = NS * part
     lines = rows // 128
 
-    def both_columns(own, other):
-        return jnp.where(hh == 0, cat(own, other), cat(other, own))
-
-    def along_z(both):
-        return lax.all_gather(both, "dp", axis=0, axis_index_groups=Z_GROUPS)
-
-    hint_both = both_columns(hint_weight, dp_send(hint_weight, 1, 0))
-    hint_weights = along_z(hint_both)
+    def along_z(x):
+        return lax.all_gather(x, "dp", axis=0, axis_index_groups=Z_GROUPS)
+
+    hint_weights = along_z(cat(hint_weight, dp_send(hint_weight, 1, 0)))
     slot = weights[0]
-    slot_other = dp_send(slot, 1, 0)
-
-    def send_main(beside):
-        half = lax.dynamic_slice_in_dim(main_stream[0], branch * part, part, 0)
-        half = after(jnp.transpose(half.reshape(part, NS, width), (1, 0, 2)), beside)
-        return lax.all_to_all(half, "seq", split_axis=0, concat_axis=0, tiled=True).reshape(rows, width)
-
-    blocks, slot_both, main_cols = relay_context(
-        context[0], slot_other, lambda slot_other: both_columns(slot, slot_other), send_main
+
+    def join_slot(other):
+        return jnp.where(hh == 0, cat(slot, other), cat(other, slot))
+
+    blocks, slot_both, main_half, where = relay_context(
+        context[0], dp_send(slot, 1, 0), join_slot, split_columns(where, main_stream[0]), where
     )
     weight = along_z(slot_both)
+    main_cols = lax.all_to_all(main_half, "seq", split_axis=0, concat_axis=0, tiled=True).reshape(rows, width)
 
     sent, kept = hint_matmul(where, blocks, hint_weights)
+    sent, main_cols = lax.optimization_barrier((sent, main_cols))
     got = core_swap(sent)
     mixed, small = mix(kept, got, main_cols, hint_bias[None, :], cell_order)
 
-    half = rows // 2
     cut_a, cut_b = thirds(rows)
     back, ahead, beside, small = lax.optimization_barrier(
         (
@@ -522,9 +522,7 @@
             lax.all_to_all(small, "seq", split_axis=0, concat_axis=0, tiled=True),
         )
     )
-    up = seq_send(cat(back[:half], beside[half:]), 1, 0)
-    down = seq_send(cat(beside[:half], ahead[half:]), -1, 0)
-    over = seq_send(cat(back[:half], ahead[half:]), 0, 1)
+    far, ahead_beside, back_beside = seq_send(back, 1, 0), seq_send(beside, -1, 0), seq_send(back, 0, 1)
     means = small[:, 0:lines].reshape(NS, rows)
     spreads = small[:, lines : 2 * lines].reshape(NS, rows)
     average = jnp.mean(means, axis=0)
@@ -536,30 +534,19 @@
     first, first_next = norm(
         where, norm_rows, mod, [mixed, back, ahead, beside], [(i, i, 0, 0, rows) for i in range(4)]
     )
-    up, down, over = lax.optimization_barrier((up, down, over))
+    tables = rope_tables(cells)
+    far, ahead_beside, back_beside, tables = lax.optimization_barrier((far, ahead_beside, back_beside, tables))
     first_got = core_swap(first)
     last = [
-        seq_send(up[:cut_a], 0, 1),
-        seq_send(cat(over[cut_a:half], up[half:cut_b]), 1, 0),
-        seq_send(over[cut_b:], -1, 0),
+        seq_send(far[:cut_a], 0, 1),
+        seq_send(back_beside[cut_a:cut_b], 1, 0),
+        seq_send(ahead_beside[cut_b:], -1, 0),
     ]
     second, second_next = norm(
-        where,
-        norm_rows,
-        mod,
-        [up, down, over],
-        [
-            (4, 0, 0, 0, half),
-            (4, 1, half, half, rows),
-            (5, 1, 0, 0, half),
-            (5, 2, half, half, rows),
-            (6, 2, 0, 0, half),
-            (6, 0, half, half, rows),
-        ],
-    )
-    tables = rope_tables(after(cells, up))
-    norm_other = core_swap(after(norm_rows, up))
-    last, second, tables, norm_other = lax.optimization_barrier((last, second, tables, norm_other))
+        where, norm_rows, mod, [far, ahead_beside, back_beside], [(4 + i, i, 0, 0, rows) for i in range(3)]
+    )
+    norm_other = core_swap(after(norm_rows, far))
+    last, second, norm_other = lax.optimization_barrier((last, second, norm_other))
     second_got = core_swap(second)
     last_got = [core_swap(piece) for piece in last]
     next_half = next_rows(where, first_next, second_next, last)

time: 191 us -> 183 us (0.958)
  local copies, waits for them, and re-layouts: 8.45 us -> 3.85 us
  waiting for transfers between devices: 59.8 us -> 57.1 us
    all_to_all x1, waiting for transfers between devices: 12.4 us -> 0.01 us  [on_device(): lax.all_to_all(main_half, 'seq', split_axis=0, concat_axis=0, tiled=True)]
    ppermute x17 -> x16, waiting for transfers between devices: 17.5 us -> 26.4 us  [seq_send(): return lax.ppermute(x, 'seq', seq_pairs(dy, dx))]
    slice x9 -> x3, local copies, waits for them, and re-layouts: 2.89 us -> 0.06 us  [the longest x1 0.02 us: on_device(): far[:cut_a]]
    ppermute x8, starting transfers between devices: 13.2 us -> 15.2 us  [core_swap(): return lax.ppermute(x, 'branch', SWAP)]
    ppermute x17 -> x16, starting transfers between devices: 19.9 us -> 18.8 us  [seq_send(): return lax.ppermute(x, 'seq', seq_pairs(dy, dx))]
  transfers between devices with their start and end apart: 32 -> 31, of which waited for: 15 -> 15; matrix products, arithmetic and copies ran while one was open for 7% -> 4% of each run, Pallas kernels for 23% -> 23%
where the time goes in v2:
time: 183 us
  waiting for transfers between devices  57.1 us (31%)
  starting transfers between devices  52.3 us (29%)
  Pallas kernels  42.5 us (23%)
  between operations  14.4 us (8%)
  other arithmetic  12.5 us (7%)
  local copies, waits for them, and re-layouts  3.85 us (2%)
    ppermute x16, waiting for transfers between devices, seq_send(): return lax.ppermute(x, 'seq', seq_pairs(dy, dx))  26.4 us
    ppermute x16, starting transfers between devices, seq_send(): return lax.ppermute(x, 'seq', seq_pairs(dy, dx))  18.8 us
    ppermute x8, starting transfers between devices, core_swap(): return lax.ppermute(x, 'branch', SWAP)  15.2 us
    pallas_call x1, Pallas kernels, project(): pl.pallas_call(functools.partial(project_kernel, counts, cuts), out_shape...  13.9 us
    all_to_all x1, waiting for transfers between devices, on_device(): lax.all_to_all(small, 'seq', split_axis=0, concat_axis=0, tiled=True)  13.2 us
    ppermute x2, waiting for transfers between devices, dp_send(): return lax.ppermute(x, 'dp', dp_pairs(dh, dz))  12.2 us
    pallas_call x1, Pallas kernels, hint_matmul(): pl.pallas_call(functools.partial(hint_kernel, rows), out_shape=[jax.Shape...  9.94 us
    pallas_call x2, Pallas kernels, norm(): pl.pallas_call(functools.partial(norm_kernel, rows, width, order, pieces)...  9.85 us
  transfers between devices with their start and end apart: 31, of which 15 were waited for; matrix products, arithmetic and copies ran while one was open for 4% of the time, Pallas kernels for 23%

profile of v2, /device:TPU:1, one launch (start us, length us, event | category | flops | bytes accessed | tf_op | source)
XLA Modules:
  0.0 182.7 jit_solution(18338901662253043176)
XLA Ops:
  7.2 3.7 %collective-permute-start.8 = (bf16[160,640]{1,0:T(8,128)(2,1)}, bf16[160,640]{1,0:T(8,128)(2,1)S(1)}, u32[]{:S(2)}, u32[]{:S(2)}) collective-permute-start(bf16[160,640]{1,0:T(8,128)(2,1)} %param.13), channel_id=1, source_target_pairs={{0,8},{1,9},{2,10},{3,11},{4,12},{5,13},{6,14},{7,15},{8,0},{9,1},... | collective-permute-start | bytes 614408 | tf_op jit(solution)/shard_map/ppermute | solution.py:44
  10.9 4.1 %collective-permute-done.8 = bf16[160,640]{1,0:T(8,128)(2,1)S(1)} collective-permute-done((bf16[160,640]{1,0:T(8,128)(2,1)}, bf16[160,640]{1,0:T(8,128)(2,1)S(1)}, u32[]{:S(2)}, u32[]{:S(2)}) %collective-permute-start.8) | collective-permute-done | bytes 204832 | tf_op jit(solution)/shard_map/ppermute | solution.py:44
  14.9 1.7 pad_maximum_fusion
  16.7 3.7 %collective-permute-start.1 = (bf16[128,2560]{1,0:T(8,128)(2,1)}, bf16[128,2560]{1,0:T(8,128)(2,1)S(1)}, u32[]{:S(2)}, u32[]{:S(2)}) collective-permute-start(bf16[128,2560]{1,0:T(8,128)(2,1)} %bitcast.35), channel_id=1, source_target_pairs={{0,96},{16,112},{32,0},{48,16},{64,32},{80,48},{96,64},{112,80},{1... | collective-permute-start | bytes 1966088 | tf_op jit(solution)/shard_map/ppermute | solution.py:40
  20.4 2.7 %collective-permute-start.2 = (bf16[320,640]{1,0:T(8,128)(2,1)}, bf16[320,640]{1,0:T(8,128)(2,1)S(1)}, u32[]{:S(2)}, u32[]{:S(2)}) collective-permute-start(bf16[320,640]{1,0:T(8,128)(2,1)} %bitcast.40), channel_id=1, source_target_pairs={{0,8},{1,9},{2,10},{3,11},{4,12},{5,13},{6,14},{7,15},{8,0},{9,1},... | collective-permute-start | bytes 1228808 | tf_op jit(solution)/shard_map/ppermute | solution.py:44
  23.1 8.1 %collective-permute-done.2 = bf16[320,640]{1,0:T(8,128)(2,1)S(1)} collective-permute-done((bf16[320,640]{1,0:T(8,128)(2,1)}, bf16[320,640]{1,0:T(8,128)(2,1)S(1)}, u32[]{:S(2)}, u32[]{:S(2)}) %collective-permute-start.2) | collective-permute-done | bytes 409632 | tf_op jit(solution)/shard_map/ppermute | solution.py:44
  31.2 1.9 %collective-permute-done.1.refs_2_ = bf16[128,2560]{1,0:T(8,128)(2,1)S(1)} collective-permute-done((bf16[128,2560]{1,0:T(8,128)(2,1)}, bf16[128,2560]{1,0:T(8,128)(2,1)S(1)}, u32[]{:S(2)}, u32[]{:S(2)}) %collective-permute-start.1) | collective-permute-done | bytes 655392 | tf_op jit(solution)/shard_map/ppermute | solution.py:40
  33.2 3.0 %collective-permute-done.refs_1_ = bf16[128,2560]{1,0:T(8,128)(2,1)S(1)} collective-permute-done((bf16[128,2560]{1,0:T(8,128)(2,1)}, bf16[128,2560]{1,0:T(8,128)(2,1)S(1)}, u32[]{:S(2)}, u32[]{:S(2)}) %collective-permute-start) | collective-permute-done | bytes 655392 | tf_op jit(solution)/shard_map/ppermute | solution.py:40
  36.2 1.2 collective-permute-start.4
  37.4 2.5 %maximum_select_fusion = bf16[640,640]{1,0:T(8,128)(2,1)} fusion(bf16[320,640]{1,0:T(8,128)(2,1)} %copy-done.19, bf16[320,640]{1,0:T(8,128)(2,1)} %bitcast.41, pred[]{:T(512)S(6)} %eq.38), kind=kLoop, calls=%fused_computation.2 | loop fusion | flops 3686400 | bytes 1638401 | tf_op jit(solution)/shard_map/jit(_where)/select_n | solution.py:503
  40.0 10.0 %collective-permute-done.4.refs_3_ = bf16[128,2560]{1,0:T(8,128)(2,1)S(1)} collective-permute-done((bf16[128,2560]{1,0:T(8,128)(2,1)}, bf16[128,2560]{1,0:T(8,128)(2,1)S(1)}, u32[]{:S(2)}, u32[]{:S(2)}) %collective-permute-start.4) | collective-permute-done | bytes 655392 | tf_op jit(solution)/shard_map/ppermute | solution.py:40
  50.0 1.9 %collective-permute-done.3.refs_4_ = bf16[128,2560]{1,0:T(8,128)(2,1)} collective-permute-done((bf16[128,2560]{1,0:T(8,128)(2,1)S(1)}, bf16[128,2560]{1,0:T(8,128)(2,1)}, u32[]{:S(2)}, u32[]{:S(2)}) %collective-permute-start.3) | collective-permute-done | bytes 655392 | tf_op jit(solution)/shard_map/ppermute | solution.py:40
  52.3 2.7 %collective-permute-start.5 = (bf16[128,2560]{1,0:T(8,128)(2,1)S(1)}, bf16[128,2560]{1,0:T(8,128)(2,1)}, u32[]{:S(2)}, u32[]{:S(2)}) collective-permute-start(bf16[128,2560]{1,0:T(8,128)(2,1)S(1)} %collective-permute-done.4.refs_3_), channel_id=1, source_target_pairs={{0,96},{16,112},{32,0},{48,16},{64,32},{80,48},{96,64},{112,80},{1... | collective-permute-start | bytes 1966088 | tf_op jit(solution)/shard_map/ppermute | solution.py:40
  55.1 1.4 split_columns.1
  56.5 8.1 %collective-permute-done.7.refs_7_ = bf16[128,2560]{1,0:T(8,128)(2,1)} collective-permute-done((bf16[128,2560]{1,0:T(8,128)(2,1)}, bf16[128,2560]{1,0:T(8,128)(2,1)}, u32[]{:S(2)}, u32[]{:S(2)}) %collective-permute-start.7) | collective-permute-done | bytes 655392 | tf_op jit(solution)/shard_map/ppermute | solution.py:40
  64.6 1.0 collective-permute-done.6.refs_6_
  65.6 4.6 %all-to-all-start = ((bf16[8,64,640]{2,1,0:T(8,128)(2,1)}), bf16[8,64,640]{2,1,0:T(8,128)(2,1)S(1)}, u32[]{:S(2)}, u32[]{:S(2)}) async-start(bf16[8,64,640]{2,1,0:T(8,128)(2,1)} %split_columns.1), calls=%async_computation | async-start | bytes 1310720 | tf_op jit(solution)/shard_map/all_to_all | solution.py:509
  70.3 9.9 %hint.1 = (f32[512,640]{1,0:T(8,128)}, f32[512,640]{1,0:T(8,128)}) custom-call(s32[11]{0:T(128)} %copy-done.8, bf16[8,320,640]{2,1,0:T(8,128)(2,1)} %bitcast.34, bf16[128,2560]{1,0:T(8,128)(2,1)} %bitcast.38, bf16[128,2560]{1,0:T(8,128)(2,1)} %copy-done.15, bf16[128,2560]{1,0:T(8,128)(2,1)} %copy-done.14, bf16[128,2560]{1,0:T(8,128)(2,1)} %copy-done.16, ...), custom_call_target="tpu_custom_call" | custom-call | flops 1 | bytes 1 | tf_op jit(solution)/shard_map/hint/pallas_call | solution.py:141
  80.2 5.8 %collective-permute-start.9 = (f32[512,640]{1,0:T(8,128)}, f32[512,640]{1,0:T(8,128)S(1)}, u32[]{:S(2)}, u32[]{:S(2)}) collective-permute-start(f32[512,640]{1,0:T(8,128)} %get-tuple-element.58), channel_id=1, source_target_pairs={{0,128},{128,0},{1,129},{129,1},{2,130},{130,2},{3,131},{131,3},{4... | collective-permute-start | bytes 3932168 | tf_op jit(solution)/shard_map/ppermute | solution.py:48
  86.0 2.9 %collective-permute-done.9.got_ref = f32[512,640]{1,0:T(8,128)S(1)} collective-permute-done((f32[512,640]{1,0:T(8,128)}, f32[512,640]{1,0:T(8,128)S(1)}, u32[]{:S(2)}, u32[]{:S(2)}) %collective-permute-start.9) | collective-permute-done | bytes 1310752 | tf_op jit(solution)/shard_map/ppermute | solution.py:48
  88.9 1.3 copy-done.1
  90.2 1.4 mix.1
  91.6 1.8 %collective-permute-start.12 = (bf16[512,640]{1,0:T(8,128)(2,1)S(1)}, bf16[512,640]{1,0:T(8,128)(2,1)S(1)}, u32[]{:S(2)}, u32[]{:S(2)}) collective-permute-start(bf16[512,640]{1,0:T(8,128)(2,1)S(1)} %get-tuple-element.60.refs_0_), channel_id=1, source_target_pairs={{0,16},{16,0},{32,48},{48,32},{64,80},{80,64},{96,112},{112,96},{1... | collective-permute-start | bytes 1966088 | tf_op jit(solution)/shard_map/ppermute | solution.py:40
  93.4 2.4 %collective-permute-start.11 = (bf16[512,640]{1,0:T(8,128)(2,1)S(1)}, bf16[512,640]{1,0:T(8,128)(2,1)S(1)}, u32[]{:S(2)}, u32[]{:S(2)}) collective-permute-start(bf16[512,640]{1,0:T(8,128)(2,1)S(1)} %get-tuple-element.60.refs_0_), channel_id=1, source_target_pairs={{0,96},{16,112},{32,0},{48,16},{64,32},{80,48},{96,64},{112,80},{1... | collective-permute-start | bytes 1966088 | tf_op jit(solution)/shard_map/ppermute | solution.py:40
  95.9 4.0 %all-to-all-start.1 = ((f32[8,16,128]{2,1,0:T(8,128)}), f32[8,16,128]{2,1,0:T(8,128)S(1)}, u32[]{:S(2)}, u32[]{:S(2)}) async-start(f32[8,16,128]{2,1,0:T(8,128)} %get-tuple-element.61), calls=%async_computation.1 | async-start | bytes 131072 | tf_op jit(solution)/shard_map/all_to_all | solution.py:522
  99.9 13.2 %all-to-all-done.1 = f32[8,16,128]{2,1,0:T(8,128)S(1)} async-done(((f32[8,16,128]{2,1,0:T(8,128)}), f32[8,16,128]{2,1,0:T(8,128)S(1)}, u32[]{:S(2)}, u32[]{:S(2)}) %all-to-all-start.1) | async-done | bytes 65568 | tf_op jit(solution)/shard_map/all_to_all | solution.py:522
  113.1 0.8 copy-done.18
  114.1 2.7 %collective-permute-start.14 = (bf16[512,640]{1,0:T(8,128)(2,1)S(1)}, bf16[512,640]{1,0:T(8,128)(2,1)S(1)}, u32[]{:S(2)}, u32[]{:S(2)}) collective-permute-start(bf16[512,640]{1,0:T(8,128)(2,1)S(1)} %collective-permute-done.12.refs_3_), channel_id=1, source_target_pairs={{0,96},{16,112},{32,0},{48,16},{64,32},{80,48},{96,64},{112,80},{1... | collective-permute-start | bytes 1966088 | tf_op jit(solution)/shard_map/ppermute | solution.py:40
  116.9 0.7 maximum_maximum_fusion.norm_ref.refs_12_
  117.5 5.4 %norm.2 = (bf16[2048,640]{1,0:T(8,128)(2,1)}, bf16[4,64,640]{2,1,0:T(8,128)(2,1)}) custom-call(s32[11]{0:T(128)} %copy-done.8, f32[8,512]{1,0:T(8,128)} %maximum_maximum_fusion.norm_ref.refs_12_, f32[8,2,640]{2,1,0:T(2,128)} %bitcast.42, bf16[512,640]{1,0:T(8,128)(2,1)} %copy-done.2, bf16[512,640]{1,0:T(8,128)(2,1)} %collective-permute-done.10.refs_1_, ...), custom_call_target="tpu_custom_call" | custom-call | flops 1 | bytes 1 | tf_op jit(solution)/shard_map/norm/pallas_call | solution.py:230
  122.9 2.8 %collective-permute-start.20 = (bf16[2048,640]{1,0:T(8,128)(2,1)}, bf16[2048,640]{1,0:T(8,128)(2,1)}, u32[]{:S(2)}, u32[]{:S(2)}) collective-permute-start(bf16[2048,640]{1,0:T(8,128)(2,1)} %get-tuple-element.66.refs_0_), channel_id=1, source_target_pairs={{0,128},{128,0},{1,129},{129,1},{2,130},{130,2},{3,131},{131,3},{4... | collective-permute-start | bytes 7864328 | tf_op jit(solution)/shard_map/ppermute | solution.py:48
  125.8 3.5 %sine_multiply_fusion = (f32[1024,128]{1,0:T(8,128)}, f32[1024,128]{1,0:T(8,128)}) fusion(f32[128]{0:T(128)S(1)} %get-tuple-element.97, f32[128]{0:T(128)S(1)} %get-tuple-element.98, s32[1024]{0:T(1024)S(1)} %get-tuple-element.96, s32[1024]{0:T(1024)S(1)} %get-tuple-element.95, s32[1024]{0:T(1024)S(1)} %get-tuple-element.94, ...), kind=kLoop, calls=%fused_computation.4 | loop fusion | flops 655360 | bytes 1062144 | tf_op jit(solution)/shard_map/mul | solution.py:467
  129.3 0.4 collective-permute-done.13.refs_0_
  129.7 1.4 collective-permute-start.16
  131.2 2.2 %collective-permute-start.18 = (bf16[192,640]{1,0:T(8,128)(2,1)S(1)}, bf16[192,640]{1,0:T(8,128)(2,1)S(1)}, u32[]{:S(2)}, u32[]{:S(2)}) collective-permute-start(bf16[192,640]{1,0:T(8,128)(2,1)S(1)} %slice.23), channel_id=1, source_target_pairs={{0,96},{16,112},{32,0},{48,16},{64,32},{80,48},{96,64},{112,80},{1... | collective-permute-start | bytes 737288 | tf_op jit(solution)/shard_map/ppermute | solution.py:40
  133.5 3.9 %collective-permute-start.19 = (f32[8,512]{1,0:T(8,128)S(1)}, f32[8,512]{1,0:T(8,128)S(1)}, u32[]{:S(2)}, u32[]{:S(2)}) collective-permute-start(f32[8,512]{1,0:T(8,128)S(1)} %copy-done.20), channel_id=1, source_target_pairs={{0,128},{128,0},{1,129},{129,1},{2,130},{130,2},{3,131},{131,3},{4... | collective-permute-start | bytes 49160 | tf_op jit(solution)/shard_map/ppermute | solution.py:48
  137.4 4.5 %norm.3 = (bf16[1536,640]{1,0:T(8,128)(2,1)}, bf16[3,64,640]{2,1,0:T(8,128)(2,1)}) custom-call(s32[11]{0:T(128)} %copy-done.8, f32[8,512]{1,0:T(8,128)} %maximum_maximum_fusion.norm_ref.refs_12_, f32[8,2,640]{2,1,0:T(2,128)} %bitcast.43, bf16[512,640]{1,0:T(8,128)(2,1)} %copy-done.11, bf16[512,640]{1,0:T(8,128)(2,1)} %copy-done.12, bf16[512,640]{1,0:T(8,128)(2,1)} %copy-done.13), custom_call_target="tpu_custom_call" | custom-call | flops 1 | bytes 1 | tf_op jit(solution)/shard_map/norm/pallas_call | solution.py:230
  142.0 1.9 %collective-permute-start.21 = (bf16[1536,640]{1,0:T(8,128)(2,1)}, bf16[1536,640]{1,0:T(8,128)(2,1)}, u32[]{:S(2)}, u32[]{:S(2)}) collective-permute-start(bf16[1536,640]{1,0:T(8,128)(2,1)} %get-tuple-element.72.refs_1_), channel_id=1, source_target_pairs={{0,128},{128,0},{1,129},{129,1},{2,130},{130,2},{3,131},{131,3},{4... | collective-permute-start | bytes 5898248 | tf_op jit(solution)/shard_map/ppermute | solution.py:48
  144.0 0.4 collective-permute-start.22
  144.6 0.9 copy-done.6
  145.5 0.7 next_rows.1
  146.3 1.4 collective-permute-done.23.refs_8_
  148.3 0.5 collective-permute-done.21.refs_6_
  149.0 13.9 %project.1 = (f32[1024,640]{1,0:T(8,128)}, f32[8,8,128]{2,1,0:T(8,128)}) custom-call(s32[11]{0:T(128)} %copy-done.8, bf16[2048,640]{1,0:T(8,128)(2,1)} %get-tuple-element.66.refs_0_, bf16[1536,640]{1,0:T(8,128)(2,1)} %get-tuple-element.72.refs_1_, bf16[192,640]{1,0:T(8,128)(2,1)} %copy-done.4, bf16[128,640]{1,0:T(8,128)(2,1)} %copy-done.7, ...), custom_call_target="tpu_custom_call" | custom-call | flops 6710886400 | bytes 19660800 | tf_op jit(solution)/shard_map/project/pallas_call | solution.py:380
  162.9 3.3 %all-to-all-start.2 = ((f32[8,8,128]{2,1,0:T(8,128)}), f32[8,8,128]{2,1,0:T(8,128)S(1)}, u32[]{:S(2)}, u32[]{:S(2)}) async-start(f32[8,8,128]{2,1,0:T(8,128)} %get-tuple-element.81), calls=%async_computation.2 | async-start | bytes 65536 | tf_op jit(solution)/shard_map/all_to_all | solution.py:558
  166.3 0.9 maximum_select_fusion.1
  167.2 5.4 %turn.1 = f32[1024,640]{1,0:T(8,128)} custom-call(s32[11]{0:T(128)} %copy-done.8, f32[1024,640]{1,0:T(8,128)} %get-tuple-element.82.proj_ref, f32[1,640]{1,0:T(1,128)} %gain_ref.1, f32[1024,128]{1,0:T(8,128)} %get-tuple-element.83.cos_ref, f32[1024,128]{1,0:T(8,128)} %get-tuple-element.84.sin_ref), custom_call_target="tpu_custom_call" | custom-call | flops 6553600 | bytes 5898240 | tf_op jit(solution)/shard_map/turn/pallas_call | solution.py:431
  172.8 3.0 %fusion = bf16[1,1,1024,640]{3,2,1,0:T(8,128)(2,1)} fusion(f32[1024,640]{1,0:T(8,128)} %turn.1, f32[1024]{0:T(1024)S(1)} %mul.71), kind=kLoop, calls=%fused_computation.1 | loop fusion | flops 1310720 | bytes 3936256 | tf_op jit(solution)/shard_map/broadcast_in_dim | solution.py:571
  (104 shorter events, 2.6 us)
Async XLA Ops:
  7.2 63.1 %all-gather.5.cloned.1.call-start = ((), (), s32[]{:S(2)}) async-start(), calls=%async_computation.3 | async-start | bytes 3686400 | tf_op jit(solution)/shard_map/all_gather | solution.py:497
  7.2 7.7 %collective-permute-start.8 = (bf16[160,640]{1,0:T(8,128)(2,1)}, bf16[160,640]{1,0:T(8,128)(2,1)S(1)}, u32[]{:S(2)}, u32[]{:S(2)}) collective-permute-start(bf16[160,640]{1,0:T(8,128)(2,1)} %param.13), channel_id=1, source_target_pairs={{0,8},{1,9},{2,10},{3,11},{4,12},{5,13},{6,14},{7,15},{8,0},{9,1},... | collective-permute-start | bytes 614408 | tf_op jit(solution)/shard_map/ppermute | solution.py:44
  16.6 38.4 %copy-start = (bf16[1,128,5120]{2,1,0:T(8,128)(2,1)S(1)}, bf16[1,128,5120]{2,1,0:T(8,128)(2,1)}, u32[]{:S(2)}) copy-start(bf16[1,128,5120]{2,1,0:T(8,128)(2,1)} %param.10) | copy-start | bytes 3932164
  16.7 129.6 %all-gather.7.cloned.1.call-start = ((), (), s32[]{:S(2)}) async-start(), calls=%async_computation.4 | async-start | bytes 7372800 | tf_op jit(solution)/shard_map/all_gather | solution.py:497
  16.7 16.5 %collective-permute-start.1 = (bf16[128,2560]{1,0:T(8,128)(2,1)}, bf16[128,2560]{1,0:T(8,128)(2,1)S(1)}, u32[]{:S(2)}, u32[]{:S(2)}) collective-permute-start(bf16[128,2560]{1,0:T(8,128)(2,1)} %bitcast.35), channel_id=1, source_target_pairs={{0,96},{16,112},{32,0},{48,16},{64,32},{80,48},{96,64},{112,80},{1... | collective-permute-start | bytes 1966088 | tf_op jit(solution)/shard_map/ppermute | solution.py:40
  20.4 15.8 %collective-permute-start = (bf16[128,2560]{1,0:T(8,128)(2,1)}, bf16[128,2560]{1,0:T(8,128)(2,1)S(1)}, u32[]{:S(2)}, u32[]{:S(2)}) collective-permute-start(bf16[128,2560]{1,0:T(8,128)(2,1)} %bitcast.36), channel_id=1, source_target_pairs={{0,32},{16,48},{32,64},{48,80},{64,96},{80,112},{96,0},{112,16},{1... | collective-permute-start | bytes 1966088 | tf_op jit(solution)/shard_map/ppermute | solution.py:40
  20.4 10.8 %collective-permute-start.2 = (bf16[320,640]{1,0:T(8,128)(2,1)}, bf16[320,640]{1,0:T(8,128)(2,1)S(1)}, u32[]{:S(2)}, u32[]{:S(2)}) collective-permute-start(bf16[320,640]{1,0:T(8,128)(2,1)} %bitcast.40), channel_id=1, source_target_pairs={{0,8},{1,9},{2,10},{3,11},{4,12},{5,13},{6,14},{7,15},{8,0},{9,1},... | collective-permute-start | bytes 1228808 | tf_op jit(solution)/shard_map/ppermute | solution.py:44
  33.2 23.3 %copy-start.14 = (bf16[128,2560]{1,0:T(8,128)(2,1)}, bf16[128,2560]{1,0:T(8,128)(2,1)S(1)}, u32[]{:S(2)}) copy-start(bf16[128,2560]{1,0:T(8,128)(2,1)S(1)} %collective-permute-done.1.refs_2_) | copy-start | bytes 1966084
  36.2 20.3 %copy-start.15 = (bf16[128,2560]{1,0:T(8,128)(2,1)}, bf16[128,2560]{1,0:T(8,128)(2,1)S(1)}, u32[]{:S(2)}) copy-start(bf16[128,2560]{1,0:T(8,128)(2,1)S(1)} %collective-permute-done.refs_1_) | copy-start | bytes 1966084
  36.2 13.8 %collective-permute-start.4 = (bf16[128,2560]{1,0:T(8,128)(2,1)}, bf16[128,2560]{1,0:T(8,128)(2,1)S(1)}, u32[]{:S(2)}, u32[]{:S(2)}) collective-permute-start(bf16[128,2560]{1,0:T(8,128)(2,1)} %bitcast.37), channel_id=1, source_target_pairs={{0,16},{16,0},{32,48},{48,32},{64,80},{80,64},{96,112},{112,96},{1... | collective-permute-start | bytes 1966088 | tf_op jit(solution)/shard_map/ppermute | solution.py:40
  37.4 14.5 %collective-permute-start.3 = (bf16[128,2560]{1,0:T(8,128)(2,1)S(1)}, bf16[128,2560]{1,0:T(8,128)(2,1)}, u32[]{:S(2)}, u32[]{:S(2)}) collective-permute-start(bf16[128,2560]{1,0:T(8,128)(2,1)S(1)} %collective-permute-done.refs_1_), channel_id=1, source_target_pairs={{0,32},{16,48},{32,64},{48,80},{64,96},{80,112},{96,0},{112,16},{1... | collective-permute-start | bytes 1966088 | tf_op jit(solution)/shard_map/ppermute | solution.py:40
  50.0 15.6 %copy-start.16 = (bf16[128,2560]{1,0:T(8,128)(2,1)}, bf16[128,2560]{1,0:T(8,128)(2,1)S(1)}, u32[]{:S(2)}) copy-start(bf16[128,2560]{1,0:T(8,128)(2,1)S(1)} %collective-permute-done.4.refs_3_) | copy-start | bytes 1966084
  52.0 12.7 %collective-permute-start.7 = (bf16[128,2560]{1,0:T(8,128)(2,1)}, bf16[128,2560]{1,0:T(8,128)(2,1)}, u32[]{:S(2)}, u32[]{:S(2)}) collective-permute-start(bf16[128,2560]{1,0:T(8,128)(2,1)} %collective-permute-done.3.refs_4_), channel_id=1, source_target_pairs={{0,16},{16,0},{32,48},{48,32},{64,80},{80,64},{96,112},{112,96},{1... | collective-permute-start | bytes 1966088 | tf_op jit(solution)/shard_map/ppermute | solution.py:40
  52.3 13.3 %collective-permute-start.6 = (bf16[128,2560]{1,0:T(8,128)(2,1)S(1)}, bf16[128,2560]{1,0:T(8,128)(2,1)}, u32[]{:S(2)}, u32[]{:S(2)}) collective-permute-start(bf16[128,2560]{1,0:T(8,128)(2,1)S(1)} %collective-permute-done.4.refs_3_), channel_id=1, source_target_pairs={{0,32},{16,48},{32,64},{48,80},{64,96},{80,112},{96,0},{112,16},{1... | collective-permute-start | bytes 1966088 | tf_op jit(solution)/shard_map/ppermute | solution.py:40
  52.3 13.3 %collective-permute-start.5 = (bf16[128,2560]{1,0:T(8,128)(2,1)S(1)}, bf16[128,2560]{1,0:T(8,128)(2,1)}, u32[]{:S(2)}, u32[]{:S(2)}) collective-permute-start(bf16[128,2560]{1,0:T(8,128)(2,1)S(1)} %collective-permute-done.4.refs_3_), channel_id=1, source_target_pairs={{0,96},{16,112},{32,0},{48,16},{64,32},{80,48},{96,64},{112,80},{1... | collective-permute-start | bytes 1966088 | tf_op jit(solution)/shard_map/ppermute | solution.py:40
  55.1 10.6 %copy-start.8 = (s32[11]{0:T(128)}, s32[11]{0:T(128)S(1)}, u32[]{:S(2)}) copy-start(s32[11]{0:T(128)S(1)} %stack.47.where_ref) | copy-start | bytes 136
  65.6 14.6 %all-to-all-start = ((bf16[8,64,640]{2,1,0:T(8,128)(2,1)}), bf16[8,64,640]{2,1,0:T(8,128)(2,1)S(1)}, u32[]{:S(2)}, u32[]{:S(2)}) async-start(bf16[8,64,640]{2,1,0:T(8,128)(2,1)} %split_columns.1), calls=%async_computation | async-start | bytes 1310720 | tf_op jit(solution)/shard_map/all_to_all | solution.py:509
  70.2 15.8 %copy-start.21 = (f32[640]{0:T(1024)S(1)}, f32[640]{0:T(1024)}, u32[]{:S(2)}) copy-start(f32[640]{0:T(1024)} %param.14) | copy-start | bytes 7684
  70.3 18.6 %copy-start.10 = (s32[1,128]{1,0:T(1,128)S(1)}, s32[1,128]{1,0:T(1,128)}, u32[]{:S(2)}) copy-start(s32[1,128]{1,0:T(1,128)} %cell_ref.1) | copy-start | bytes 1540
  80.2 8.7 %collective-permute-start.9 = (f32[512,640]{1,0:T(8,128)}, f32[512,640]{1,0:T(8,128)S(1)}, u32[]{:S(2)}, u32[]{:S(2)}) collective-permute-start(f32[512,640]{1,0:T(8,128)} %get-tuple-element.58), channel_id=1, source_target_pairs={{0,128},{128,0},{1,129},{129,1},{2,130},{130,2},{3,131},{131,3},{4... | collective-permute-start | bytes 3932168 | tf_op jit(solution)/shard_map/ppermute | solution.py:48
  91.6 26.0 %copy-start.2 = (bf16[512,640]{1,0:T(8,128)(2,1)}, bf16[512,640]{1,0:T(8,128)(2,1)S(1)}, u32[]{:S(2)}) copy-start(bf16[512,640]{1,0:T(8,128)(2,1)S(1)} %get-tuple-element.60.refs_0_) | copy-start | bytes 1966084
  91.6 21.5 %collective-permute-start.12 = (bf16[512,640]{1,0:T(8,128)(2,1)S(1)}, bf16[512,640]{1,0:T(8,128)(2,1)S(1)}, u32[]{:S(2)}, u32[]{:S(2)}) collective-permute-start(bf16[512,640]{1,0:T(8,128)(2,1)S(1)} %get-tuple-element.60.refs_0_), channel_id=1, source_target_pairs={{0,16},{16,0},{32,48},{48,32},{64,80},{80,64},{96,112},{112,96},{1... | collective-permute-start | bytes 1966088 | tf_op jit(solution)/shard_map/ppermute | solution.py:40
  93.4 19.6 %collective-permute-start.11 = (bf16[512,640]{1,0:T(8,128)(2,1)S(1)}, bf16[512,640]{1,0:T(8,128)(2,1)S(1)}, u32[]{:S(2)}, u32[]{:S(2)}) collective-permute-start(bf16[512,640]{1,0:T(8,128)(2,1)S(1)} %get-tuple-element.60.refs_0_), channel_id=1, source_target_pairs={{0,96},{16,112},{32,0},{48,16},{64,32},{80,48},{96,64},{112,80},{1... | collective-permute-start | bytes 1966088 | tf_op jit(solution)/shard_map/ppermute | solution.py:40
  95.8 17.3 %collective-permute-start.10 = (bf16[512,640]{1,0:T(8,128)(2,1)S(1)}, bf16[512,640]{1,0:T(8,128)(2,1)}, u32[]{:S(2)}, u32[]{:S(2)}) collective-permute-start(bf16[512,640]{1,0:T(8,128)(2,1)S(1)} %get-tuple-element.60.refs_0_), channel_id=1, source_target_pairs={{0,32},{16,48},{32,64},{48,80},{64,96},{80,112},{96,0},{112,16},{1... | collective-permute-start | bytes 1966088 | tf_op jit(solution)/shard_map/ppermute | solution.py:40
  95.9 17.1 %all-to-all-start.1 = ((f32[8,16,128]{2,1,0:T(8,128)}), f32[8,16,128]{2,1,0:T(8,128)S(1)}, u32[]{:S(2)}, u32[]{:S(2)}) async-start(f32[8,16,128]{2,1,0:T(8,128)} %get-tuple-element.61), calls=%async_computation.1 | async-start | bytes 131072 | tf_op jit(solution)/shard_map/all_to_all | solution.py:522
  113.9 15.4 %collective-permute-start.15 = (bf16[512,640]{1,0:T(8,128)(2,1)}, bf16[512,640]{1,0:T(8,128)(2,1)S(1)}, u32[]{:S(2)}, u32[]{:S(2)}) collective-permute-start(bf16[512,640]{1,0:T(8,128)(2,1)} %collective-permute-done.10.refs_1_), channel_id=1, source_target_pairs={{0,16},{16,0},{32,48},{48,32},{64,80},{80,64},{96,112},{112,96},{1... | collective-permute-start | bytes 1966088 | tf_op jit(solution)/shard_map/ppermute | solution.py:40
  114.1 15.5 %collective-permute-start.13 = (bf16[512,640]{1,0:T(8,128)(2,1)}, bf16[512,640]{1,0:T(8,128)(2,1)S(1)}, u32[]{:S(2)}, u32[]{:S(2)}) collective-permute-start(bf16[512,640]{1,0:T(8,128)(2,1)} %collective-permute-done.10.refs_1_), channel_id=1, source_target_pairs={{0,32},{16,48},{32,64},{48,80},{64,96},{80,112},{96,0},{112,16},{1... | collective-permute-start | bytes 1966088 | tf_op jit(solution)/shard_map/ppermute | solution.py:40
  114.1 15.2 %collective-permute-start.14 = (bf16[512,640]{1,0:T(8,128)(2,1)S(1)}, bf16[512,640]{1,0:T(8,128)(2,1)S(1)}, u32[]{:S(2)}, u32[]{:S(2)}) collective-permute-start(bf16[512,640]{1,0:T(8,128)(2,1)S(1)} %collective-permute-done.12.refs_3_), channel_id=1, source_target_pairs={{0,96},{16,112},{32,0},{48,16},{64,32},{80,48},{96,64},{112,80},{1... | collective-permute-start | bytes 1966088 | tf_op jit(solution)/shard_map/ppermute | solution.py:40
  122.9 10.6 %copy-start.20 = (f32[8,512]{1,0:T(8,128)S(1)}, f32[8,512]{1,0:T(8,128)}, u32[]{:S(2)}) copy-start(f32[8,512]{1,0:T(8,128)} %maximum_maximum_fusion.norm_ref.refs_12_) | copy-start | bytes 49156
  122.9 25.4 %collective-permute-start.20 = (bf16[2048,640]{1,0:T(8,128)(2,1)}, bf16[2048,640]{1,0:T(8,128)(2,1)}, u32[]{:S(2)}, u32[]{:S(2)}) collective-permute-start(bf16[2048,640]{1,0:T(8,128)(2,1)} %get-tuple-element.66.refs_0_), channel_id=1, source_target_pairs={{0,128},{128,0},{1,129},{129,1},{2,130},{130,2},{3,131},{131,3},{4... | collective-permute-start | bytes 7864328 | tf_op jit(solution)/shard_map/ppermute | solution.py:48
  129.3 8.1 %copy-start.12 = (bf16[512,640]{1,0:T(8,128)(2,1)}, bf16[512,640]{1,0:T(8,128)(2,1)S(1)}, u32[]{:S(2)}) copy-start(bf16[512,640]{1,0:T(8,128)(2,1)S(1)} %collective-permute-done.14.refs_1_) | copy-start | bytes 1966084
  129.3 8.1 %copy-start.13 = (bf16[512,640]{1,0:T(8,128)(2,1)}, bf16[512,640]{1,0:T(8,128)(2,1)S(1)}, u32[]{:S(2)}) copy-start(bf16[512,640]{1,0:T(8,128)(2,1)S(1)} %collective-permute-done.15.refs_2_) | copy-start | bytes 1966084
  129.7 7.7 %copy-start.11 = (bf16[512,640]{1,0:T(8,128)(2,1)}, bf16[512,640]{1,0:T(8,128)(2,1)S(1)}, u32[]{:S(2)}) copy-start(bf16[512,640]{1,0:T(8,128)(2,1)S(1)} %collective-permute-done.13.refs_0_) | copy-start | bytes 1966084
  129.7 14.9 %copy-start.3 = (bf16[4,64,640]{2,1,0:T(8,128)(2,1)S(1)}, bf16[4,64,640]{2,1,0:T(8,128)(2,1)}, u32[]{:S(2)}) copy-start(bf16[4,64,640]{2,1,0:T(8,128)(2,1)} %get-tuple-element.77.first_ref) | copy-start | bytes 983044
  129.7 14.9 %copy-start.9 = (s32[11]{0:T(128)S(1)}, s32[11]{0:T(128)}, u32[]{:S(2)}) copy-start(s32[11]{0:T(128)} %copy-done.8) | copy-start | bytes 136
  129.7 12.2 %collective-permute-start.16 = (bf16[192,640]{1,0:T(8,128)(2,1)S(1)}, bf16[192,640]{1,0:T(8,128)(2,1)S(1)}, u32[]{:S(2)}, u32[]{:S(2)}) collective-permute-start(bf16[192,640]{1,0:T(8,128)(2,1)S(1)} %slice.21), channel_id=1, source_target_pairs={{0,16},{16,0},{32,48},{48,32},{64,80},{80,64},{96,112},{112,96},{1... | collective-permute-start | bytes 737288 | tf_op jit(solution)/shard_map/ppermute | solution.py:40
  131.2 10.8 %collective-permute-start.18 = (bf16[192,640]{1,0:T(8,128)(2,1)S(1)}, bf16[192,640]{1,0:T(8,128)(2,1)S(1)}, u32[]{:S(2)}, u32[]{:S(2)}) collective-permute-start(bf16[192,640]{1,0:T(8,128)(2,1)S(1)} %slice.23), channel_id=1, source_target_pairs={{0,96},{16,112},{32,0},{48,16},{64,32},{80,48},{96,64},{112,80},{1... | collective-permute-start | bytes 737288 | tf_op jit(solution)/shard_map/ppermute | solution.py:40
  133.4 8.5 %collective-permute-start.17 = (bf16[128,640]{1,0:T(8,128)(2,1)S(1)}, bf16[128,640]{1,0:T(8,128)(2,1)S(1)}, u32[]{:S(2)}, u32[]{:S(2)}) collective-permute-start(bf16[128,640]{1,0:T(8,128)(2,1)S(1)} %slice.22), channel_id=1, source_target_pairs={{0,32},{16,48},{32,64},{48,80},{64,96},{80,112},{96,0},{112,16},{1... | collective-permute-start | bytes 491528 | tf_op jit(solution)/shard_map/ppermute | solution.py:40
  133.5 8.4 %collective-permute-start.19 = (f32[8,512]{1,0:T(8,128)S(1)}, f32[8,512]{1,0:T(8,128)S(1)}, u32[]{:S(2)}, u32[]{:S(2)}) collective-permute-start(f32[8,512]{1,0:T(8,128)S(1)} %copy-done.20), channel_id=1, source_target_pairs={{0,128},{128,0},{1,129},{129,1},{2,130},{130,2},{3,131},{131,3},{4... | collective-permute-start | bytes 49160 | tf_op jit(solution)/shard_map/ppermute | solution.py:48
  141.9 6.9 %copy-start.25 = (f32[8,512]{1,0:T(8,128)}, f32[8,512]{1,0:T(8,128)S(1)}, u32[]{:S(2)}) copy-start(f32[8,512]{1,0:T(8,128)S(1)} %collective-permute-done.19.refs_13_) | copy-start | bytes 49156
  141.9 6.9 %copy-start.7 = (bf16[128,640]{1,0:T(8,128)(2,1)}, bf16[128,640]{1,0:T(8,128)(2,1)S(1)}, u32[]{:S(2)}) copy-start(bf16[128,640]{1,0:T(8,128)(2,1)S(1)} %collective-permute-done.17.refs_1_.refs_3_) | copy-start | bytes 491524
  142.0 6.9 %copy-start.4 = (bf16[192,640]{1,0:T(8,128)(2,1)}, bf16[192,640]{1,0:T(8,128)(2,1)S(1)}, u32[]{:S(2)}) copy-start(bf16[192,640]{1,0:T(8,128)(2,1)S(1)} %collective-permute-done.16.refs_0_.refs_2_) | copy-start | bytes 737284
  142.0 6.8 %collective-permute-start.21 = (bf16[1536,640]{1,0:T(8,128)(2,1)}, bf16[1536,640]{1,0:T(8,128)(2,1)}, u32[]{:S(2)}, u32[]{:S(2)}) collective-permute-start(bf16[1536,640]{1,0:T(8,128)(2,1)} %get-tuple-element.72.refs_1_), channel_id=1, source_target_pairs={{0,128},{128,0},{1,129},{129,1},{2,130},{130,2},{3,131},{131,3},{4... | collective-permute-start | bytes 5898248 | tf_op jit(solution)/shard_map/ppermute | solution.py:48
  143.9 3.7 %collective-permute-start.23 = (bf16[128,640]{1,0:T(8,128)(2,1)S(1)}, bf16[128,640]{1,0:T(8,128)(2,1)S(1)}, u32[]{:S(2)}, u32[]{:S(2)}) collective-permute-start(bf16[128,640]{1,0:T(8,128)(2,1)S(1)} %collective-permute-done.17.refs_1_.refs_3_), channel_id=1, source_target_pairs={{0,128},{128,0},{1,129},{129,1},{2,130},{130,2},{3,131},{131,3},{4... | collective-permute-start | bytes 491528 | tf_op jit(solution)/shard_map/ppermute | solution.py:48
  144.0 3.9 %collective-permute-start.22 = (bf16[192,640]{1,0:T(8,128)(2,1)S(1)}, bf16[192,640]{1,0:T(8,128)(2,1)S(1)}, u32[]{:S(2)}, u32[]{:S(2)}) collective-permute-start(bf16[192,640]{1,0:T(8,128)(2,1)S(1)} %collective-permute-done.16.refs_0_.refs_2_), channel_id=1, source_target_pairs={{0,128},{128,0},{1,129},{129,1},{2,130},{130,2},{3,131},{131,3},{4... | collective-permute-start | bytes 737288 | tf_op jit(solution)/shard_map/ppermute | solution.py:48
  144.4 3.9 %collective-permute-start.24 = (bf16[192,640]{1,0:T(8,128)(2,1)S(1)}, bf16[192,640]{1,0:T(8,128)(2,1)S(1)}, u32[]{:S(2)}, u32[]{:S(2)}) collective-permute-start(bf16[192,640]{1,0:T(8,128)(2,1)S(1)} %collective-permute-done.18.refs_2_.refs_4_), channel_id=1, source_target_pairs={{0,128},{128,0},{1,129},{129,1},{2,130},{130,2},{3,131},{131,3},{4... | collective-permute-start | bytes 737288 | tf_op jit(solution)/shard_map/ppermute | solution.py:48
  147.6 18.6 %collective-permute-start.25 = (bf16[64,2560]{1,0:T(8,128)(2,1)S(1)}, bf16[64,2560]{1,0:T(8,128)(2,1)S(1)}, u32[]{:S(2)}, u32[]{:S(2)}) collective-permute-start(bf16[64,2560]{1,0:T(8,128)(2,1)S(1)} %get-tuple-element.91), channel_id=1, source_target_pairs={{0,128},{128,0},{1,129},{129,1},{2,130},{130,2},{3,131},{131,3},{4... | collective-permute-start | bytes 983048 | tf_op jit(solution)/shard_map/ppermute | solution.py:48
  162.9 9.7 %all-to-all-start.2 = ((f32[8,8,128]{2,1,0:T(8,128)}), f32[8,8,128]{2,1,0:T(8,128)S(1)}, u32[]{:S(2)}, u32[]{:S(2)}) async-start(f32[8,8,128]{2,1,0:T(8,128)} %get-tuple-element.81), calls=%async_computation.2 | async-start | bytes 65536 | tf_op jit(solution)/shard_map/all_to_all | solution.py:558
  (9 other events, 19.1 us)
Sparse Core Ops, SparseCore 0:
  16.8 50.9 all-gather.4
  69.5 75.5 all-gather.6

commit v3 on v2

--- a/solution.py
+++ b/solution.py
@@ -404,39 +404,73 @@
     )(where, *operands, bias, norm_rows, norm_other, mod)
 
 
-def turn_kernel(where_ref, proj_ref, gain_ref, cos_ref, sin_ref, out_ref):
-    tokens, columns = out_ref.shape
-    part = tokens // 2 // NS
+def turn_kernel(
+    where_ref, proj_ref, next_ref, got_ref, gain_ref, cos_ref, sin_ref, out_ref, placed_ref,
+    held, done, near, load_sem, store_sem, near_sem,
+):
+    chunks, step, columns = held.shape
+    part = proj_ref.shape[0] // 2 // NS
+    loads = [pltpu.make_async_copy(proj_ref.at[pl.ds(k * step, step)], held.at[k], load_sem.at[k]) for k in range(chunks)]
+    for c in loads:
+        c.start()
     mine = where_ref[8]
+    tokens = near.shape[1]
+    fetches, places = [], []
+    for h, (src, half) in enumerate(((next_ref.at[mine], mine), (got_ref, 1 - mine))):
+        at = pl.ds(pl.multiple_of(half * tokens, 16), tokens)
+        fetches.append(pltpu.make_async_copy(src, near.at[h], near_sem.at[h]))
+        places.append(pltpu.make_async_copy(near.at[h], placed_ref.at[at], near_sem.at[2 + h]))
+    for c in fetches:
+        c.start()
     even = lax.broadcasted_iota(jnp.int32, (part, HEAD), 1) % 2 == 0
-
-    def body(s, _):
-        for h in range(2):
-            half = mine if h == 0 else 1 - mine
-            src = pl.ds(pl.multiple_of((h * NS + s) * part, 16), part)
+    stores = []
+    for k in range(chunks):
+        half = mine if k < chunks // 2 else 1 - mine
+        if k == chunks // 2:
+            for fetch, place in zip(fetches, places):
+                fetch.wait()
+                place.start()
+        loads[k].wait()
+        for j in range(step // part):
+            s = k % (chunks // 2) * (step // part) + j
+            src = slice(j * part, (j + 1) * part)
             dst = pl.ds(pl.multiple_of((2 * s + half) * part, 16), part)
             cosine, sine = cos_ref[dst, :], sin_ref[dst, :]
             for a in range(columns // HEAD):
                 lanes = slice(a * HEAD, (a + 1) * HEAD)
-                value = proj_ref[src, lanes] * gain_ref[:, lanes]
+                value = held[k, src, lanes] * gain_ref[:, lanes]
                 partner = jnp.where(even, pltpu.roll(value, HEAD - 1, 1), pltpu.roll(value, 1, 1))
-                out_ref[dst, lanes] = value * cosine + partner * sine
-        return 0
-
-    lax.fori_loop(0, NS, body, 0)
-
-
-def turn(where, proj, gain, cosine, sine):
+                done[k, src, lanes] = value * cosine + partner * sine
+            c = pltpu.make_async_copy(done.at[k, pl.ds(j * part, part)], out_ref.at[dst], store_sem.at[len(stores)])
+            c.start()
+            stores.append(c)
+    for c in stores + places:
+        c.wait()
+
+
+def turn(where, proj, next_half, next_got, gain, cosine, sine):
     tokens, columns = proj.shape
+    chunks = 8
     return pl.pallas_call(
         turn_kernel,
-        out_shape=jax.ShapeDtypeStruct((tokens, columns), F32),
-        in_specs=[SCALARS] + [WHOLE] * 4,
-        out_specs=WHOLE,
+        out_shape=[
+            jax.ShapeDtypeStruct((tokens, columns), F32),
+            jax.ShapeDtypeStruct((2 * next_got.shape[0], next_got.shape[1]), BF16),
+        ],
+        in_specs=[SCALARS] + [HBM] * 3 + [WHOLE] * 3,
+        out_specs=[HBM] * 2,
+        scratch_shapes=[
+            pltpu.VMEM((chunks, tokens // chunks, columns), F32),
+            pltpu.VMEM((chunks, tokens // chunks, columns), F32),
+            pltpu.VMEM((2, *next_got.shape), BF16),
+            pltpu.SemaphoreType.DMA((chunks,)),
+            pltpu.SemaphoreType.DMA((2 * NS,)),
+            pltpu.SemaphoreType.DMA((4,)),
+        ],
         compiler_params=pltpu.CompilerParams(vmem_limit_bytes=60 * MIB),
         cost_estimate=pl.CostEstimate(flops=10 * tokens * columns, bytes_accessed=9 * tokens * columns, transcendentals=0),
         name="turn",
-    )(where, proj, gain, cosine, sine)
+    )(where, proj, next_half, next_got, gain, cosine, sine)
 
 
 def rope_tables(cell_ids):
@@ -556,14 +590,11 @@
         where, [first, second, *last], [first_got, second_got, *last_got], weight, biases, norm_rows, norm_other, mod
     )
     squares = lax.all_to_all(squares, "seq", split_axis=0, concat_axis=0, tiled=True)
-    turned = turn(where, proj, norm_gains, *tables)
-
-    next_mine = lax.dynamic_index_in_dim(next_half, branch, 0, keepdims=False)
+
     next_sent = lax.dynamic_index_in_dim(next_half, 1 - branch, 0, keepdims=False)
-    next_got = core_swap(next_sent)
-    main_next = jnp.where(branch == 0, cat(next_mine, next_got), cat(next_got, next_mine))
-
-    squares, main_next, turned = lax.optimization_barrier((squares, main_next, turned))
+    turned, main_next = turn(where, proj, next_half, core_swap(next_sent), norm_gains, *tables)
+
+    squares, turned = lax.optimization_barrier((squares, turned))
     inv_rms = lax.rsqrt(jnp.sum(squares, axis=0) / features + norm_eps).reshape(2, NS, part)
     inv_rms = jnp.where(branch == 0, inv_rms, inv_rms[::-1])
     inv_rms = jnp.transpose(inv_rms, (1, 0, 2)).reshape(NS * tokens)

time: 183 us -> 182 us (level)
  waiting for transfers between devices: 57.1 us -> 55.2 us
    all_gather x2, waiting for transfers between devices: 0.03 us -> 2.75 us  [along_z(): return lax.all_gather(x, 'dp', axis=0, axis_index_groups=Z_GROUPS)]
    ppermute x8, waiting for transfers between devices: 5.28 us -> 2.88 us  [core_swap(): return lax.ppermute(x, 'branch', SWAP)]
    unnamed x52 -> x50, local copies, waits for them, and re-layouts: 3.41 us -> 4.64 us
  transfers between devices with their start and end apart: 31 -> 31, of which waited for: 15 -> 11; matrix products, arithmetic and copies ran while one was open for 4% -> 4% of each run, Pallas kernels for 23% -> 23%
where the time goes in v3:
time: 182 us; the launch traced here: 181 us
  waiting for transfers between devices  55.2 us (30%)
  starting transfers between devices  52.9 us (29%)
  Pallas kernels  42.2 us (23%)
  between operations  14.5 us (8%)
  other arithmetic  11.4 us (6%)
  local copies, waits for them, and re-layouts  5.06 us (3%)
    ppermute x16, waiting for transfers between devices, seq_send(): return lax.ppermute(x, 'seq', seq_pairs(dy, dx))  26.2 us
    ppermute x16, starting transfers between devices, seq_send(): return lax.ppermute(x, 'seq', seq_pairs(dy, dx))  18.8 us
    ppermute x8, starting transfers between devices, core_swap(): return lax.ppermute(x, 'branch', SWAP)  15.8 us
    pallas_call x1, Pallas kernels, project(): pl.pallas_call(functools.partial(project_kernel, counts, cuts), out_shape...  13.9 us
    all_to_all x1, waiting for transfers between devices, on_device(): lax.all_to_all(small, 'seq', split_axis=0, concat_axis=0, tiled=True)  12 us
    ppermute x2, waiting for transfers between devices, dp_send(): return lax.ppermute(x, 'dp', dp_pairs(dh, dz))  11.4 us
    pallas_call x1, Pallas kernels, hint_matmul(): pl.pallas_call(functools.partial(hint_kernel, rows), out_shape=[jax.Shape...  9.94 us
    pallas_call x2, Pallas kernels, norm(): pl.pallas_call(functools.partial(norm_kernel, rows, width, order, pieces)...  9.85 us
  transfers between devices with their start and end apart: 31, of which 11 were waited for; matrix products, arithmetic and copies ran while one was open for 4% of the time, Pallas kernels for 23%

profile of v3, /device:TPU:1, one launch (start us, length us, event | category | flops | bytes accessed | tf_op | source)
XLA Modules:
  0.0 181.3 jit_solution(10894645759933038339)
XLA Ops:
  7.2 3.7 %collective-permute-start.8 = (bf16[160,640]{1,0:T(8,128)(2,1)}, bf16[160,640]{1,0:T(8,128)(2,1)S(1)}, u32[]{:S(2)}, u32[]{:S(2)}) collective-permute-start(bf16[160,640]{1,0:T(8,128)(2,1)} %param.13), channel_id=1, source_target_pairs={{0,8},{1,9},{2,10},{3,11},{4,12},{5,13},{6,14},{7,15},{8,0},{9,1},... | collective-permute-start | bytes 614408 | tf_op jit(solution)/shard_map/ppermute | solution.py:44
  10.9 4.1 %collective-permute-done.8 = bf16[160,640]{1,0:T(8,128)(2,1)S(1)} collective-permute-done((bf16[160,640]{1,0:T(8,128)(2,1)}, bf16[160,640]{1,0:T(8,128)(2,1)S(1)}, u32[]{:S(2)}, u32[]{:S(2)}) %collective-permute-start.8) | collective-permute-done | bytes 204832 | tf_op jit(solution)/shard_map/ppermute | solution.py:44
  14.9 1.7 pad_maximum_fusion
  16.7 2.2 %collective-permute-start = (bf16[128,2560]{1,0:T(8,128)(2,1)}, bf16[128,2560]{1,0:T(8,128)(2,1)S(1)}, u32[]{:S(2)}, u32[]{:S(2)}) collective-permute-start(bf16[128,2560]{1,0:T(8,128)(2,1)} %bitcast.33), channel_id=1, source_target_pairs={{0,32},{16,48},{32,64},{48,80},{64,96},{80,112},{96,0},{112,16},{1... | collective-permute-start | bytes 1966088 | tf_op jit(solution)/shard_map/ppermute | solution.py:40
  19.0 1.5 collective-permute-start.1
  20.5 2.7 %collective-permute-start.2 = (bf16[320,640]{1,0:T(8,128)(2,1)}, bf16[320,640]{1,0:T(8,128)(2,1)S(1)}, u32[]{:S(2)}, u32[]{:S(2)}) collective-permute-start(bf16[320,640]{1,0:T(8,128)(2,1)} %bitcast.37), channel_id=1, source_target_pairs={{0,8},{1,9},{2,10},{3,11},{4,12},{5,13},{6,14},{7,15},{8,0},{9,1},... | collective-permute-start | bytes 1228808 | tf_op jit(solution)/shard_map/ppermute | solution.py:44
  23.2 7.3 %collective-permute-done.2 = bf16[320,640]{1,0:T(8,128)(2,1)S(1)} collective-permute-done((bf16[320,640]{1,0:T(8,128)(2,1)}, bf16[320,640]{1,0:T(8,128)(2,1)S(1)}, u32[]{:S(2)}, u32[]{:S(2)}) %collective-permute-start.2) | collective-permute-done | bytes 409632 | tf_op jit(solution)/shard_map/ppermute | solution.py:44
  30.5 2.7 %collective-permute-done.refs_1_ = bf16[128,2560]{1,0:T(8,128)(2,1)S(1)} collective-permute-done((bf16[128,2560]{1,0:T(8,128)(2,1)}, bf16[128,2560]{1,0:T(8,128)(2,1)S(1)}, u32[]{:S(2)}, u32[]{:S(2)}) %collective-permute-start) | collective-permute-done | bytes 655392 | tf_op jit(solution)/shard_map/ppermute | solution.py:40
  33.6 1.6 collective-permute-start.4
  35.2 0.9 collective-permute-start.3
  36.1 2.4 %maximum_select_fusion = bf16[640,640]{1,0:T(8,128)(2,1)} fusion(bf16[320,640]{1,0:T(8,128)(2,1)S(1)} %collective-permute-done.2, bf16[320,640]{1,0:T(8,128)(2,1)} %bitcast.38, pred[]{:T(512)S(6)} %eq.37), kind=kLoop, calls=%fused_computation.2 | loop fusion | flops 3686400 | bytes 1638401 | tf_op jit(solution)/shard_map/jit(_where)/select_n | solution.py:537
  38.4 9.2 %collective-permute-done.4.refs_3_ = bf16[128,2560]{1,0:T(8,128)(2,1)} collective-permute-done((bf16[128,2560]{1,0:T(8,128)(2,1)}, bf16[128,2560]{1,0:T(8,128)(2,1)}, u32[]{:S(2)}, u32[]{:S(2)}) %collective-permute-start.4) | collective-permute-done | bytes 655392 | tf_op jit(solution)/shard_map/ppermute | solution.py:40
  47.6 2.4 %collective-permute-done.3.refs_4_ = bf16[128,2560]{1,0:T(8,128)(2,1)} collective-permute-done((bf16[128,2560]{1,0:T(8,128)(2,1)S(1)}, bf16[128,2560]{1,0:T(8,128)(2,1)}, u32[]{:S(2)}, u32[]{:S(2)}) %collective-permute-start.3) | collective-permute-done | bytes 655392 | tf_op jit(solution)/shard_map/ppermute | solution.py:40
  50.1 1.1 collective-permute-start.5
  51.8 1.4 split_columns.1
  53.3 9.8 %collective-permute-done.5.refs_5_ = bf16[128,2560]{1,0:T(8,128)(2,1)} collective-permute-done((bf16[128,2560]{1,0:T(8,128)(2,1)}, bf16[128,2560]{1,0:T(8,128)(2,1)}, u32[]{:S(2)}, u32[]{:S(2)}) %collective-permute-start.5) | collective-permute-done | bytes 655392 | tf_op jit(solution)/shard_map/ppermute | solution.py:40
  63.1 1.7 collective-permute-done.6.refs_6_
  64.8 3.5 %all-to-all-start = ((bf16[8,64,640]{2,1,0:T(8,128)(2,1)}), bf16[8,64,640]{2,1,0:T(8,128)(2,1)S(1)}, u32[]{:S(2)}, u32[]{:S(2)}) async-start(bf16[8,64,640]{2,1,0:T(8,128)(2,1)} %split_columns.1), calls=%async_computation | async-start | bytes 1310720 | tf_op jit(solution)/shard_map/all_to_all | solution.py:543
  68.4 9.9 %hint.1 = (f32[512,640]{1,0:T(8,128)}, f32[512,640]{1,0:T(8,128)}) custom-call(s32[11]{0:T(128)} %copy-done.9, bf16[8,320,640]{2,1,0:T(8,128)(2,1)} %bitcast.32, bf16[128,2560]{1,0:T(8,128)(2,1)} %bitcast.36, bf16[128,2560]{1,0:T(8,128)(2,1)} %copy-done.15, bf16[128,2560]{1,0:T(8,128)(2,1)} %copy-done.16, bf16[128,2560]{1,0:T(8,128)(2,1)} %collective-permute-done.4.refs_3_, ...), custom_call_target="tpu_custom_call" | custom-call | flops 1 | bytes 1 | tf_op jit(solution)/shard_map/hint/pallas_call | solution.py:141
  78.3 5.2 %collective-permute-start.9 = (f32[512,640]{1,0:T(8,128)}, f32[512,640]{1,0:T(8,128)S(1)}, u32[]{:S(2)}, u32[]{:S(2)}) collective-permute-start(f32[512,640]{1,0:T(8,128)} %get-tuple-element.59), channel_id=1, source_target_pairs={{0,128},{128,0},{1,129},{129,1},{2,130},{130,2},{3,131},{131,3},{4... | collective-permute-start | bytes 3932168 | tf_op jit(solution)/shard_map/ppermute | solution.py:48
  83.6 2.9 %collective-permute-done.9.got_ref = f32[512,640]{1,0:T(8,128)S(1)} collective-permute-done((f32[512,640]{1,0:T(8,128)}, f32[512,640]{1,0:T(8,128)S(1)}, u32[]{:S(2)}, u32[]{:S(2)}) %collective-permute-start.9) | collective-permute-done | bytes 1310752 | tf_op jit(solution)/shard_map/ppermute | solution.py:48
  86.4 1.3 copy-done.2
  87.8 1.4 mix.1
  89.1 1.7 collective-permute-start.10
  90.8 1.2 collective-permute-start.11
  92.1 1.4 collective-permute-start.12
  93.6 3.4 %all-to-all-start.1 = ((f32[8,16,128]{2,1,0:T(8,128)}), f32[8,16,128]{2,1,0:T(8,128)S(1)}, u32[]{:S(2)}, u32[]{:S(2)}) async-start(f32[8,16,128]{2,1,0:T(8,128)} %get-tuple-element.62), calls=%async_computation.1 | async-start | bytes 131072 | tf_op jit(solution)/shard_map/all_to_all | solution.py:556
  97.0 12.0 %all-to-all-done.1 = f32[8,16,128]{2,1,0:T(8,128)S(1)} async-done(((f32[8,16,128]{2,1,0:T(8,128)}), f32[8,16,128]{2,1,0:T(8,128)S(1)}, u32[]{:S(2)}, u32[]{:S(2)}) %all-to-all-start.1) | async-done | bytes 65568 | tf_op jit(solution)/shard_map/all_to_all | solution.py:556
  109.0 0.8 copy-done.17
  109.8 0.7 collective-permute-start.13
  110.5 1.1 collective-permute-start.15
  111.6 2.2 %collective-permute-start.14 = (bf16[512,640]{1,0:T(8,128)(2,1)}, bf16[512,640]{1,0:T(8,128)(2,1)S(1)}, u32[]{:S(2)}, u32[]{:S(2)}) collective-permute-start(bf16[512,640]{1,0:T(8,128)(2,1)} %collective-permute-done.12.refs_3_), channel_id=1, source_target_pairs={{0,96},{16,112},{32,0},{48,16},{64,32},{80,48},{96,64},{112,80},{1... | collective-permute-start | bytes 1966088 | tf_op jit(solution)/shard_map/ppermute | solution.py:40
  113.8 0.7 maximum_maximum_fusion.norm_ref.refs_12_
  114.5 5.3 %norm.2 = (bf16[2048,640]{1,0:T(8,128)(2,1)}, bf16[4,64,640]{2,1,0:T(8,128)(2,1)}) custom-call(s32[11]{0:T(128)} %copy-done.9, f32[8,512]{1,0:T(8,128)} %maximum_maximum_fusion.norm_ref.refs_12_, f32[8,2,640]{2,1,0:T(2,128)} %bitcast.39, bf16[512,640]{1,0:T(8,128)(2,1)} %copy-done.3, bf16[512,640]{1,0:T(8,128)(2,1)} %collective-permute-done.10.refs_1_, ...), custom_call_target="tpu_custom_call" | custom-call | flops 1 | bytes 1 | tf_op jit(solution)/shard_map/norm/pallas_call | solution.py:230
  119.8 3.2 %collective-permute-start.20 = (bf16[2048,640]{1,0:T(8,128)(2,1)}, bf16[2048,640]{1,0:T(8,128)(2,1)}, u32[]{:S(2)}, u32[]{:S(2)}) collective-permute-start(bf16[2048,640]{1,0:T(8,128)(2,1)} %get-tuple-element.67.refs_0_), channel_id=1, source_target_pairs={{0,128},{128,0},{1,129},{129,1},{2,130},{130,2},{3,131},{131,3},{4... | collective-permute-start | bytes 7864328 | tf_op jit(solution)/shard_map/ppermute | solution.py:48
  123.0 3.5 %sine_multiply_fusion = (f32[1024,128]{1,0:T(8,128)}, f32[1024,128]{1,0:T(8,128)}) fusion(f32[128]{0:T(128)S(1)} %get-tuple-element.97, f32[128]{0:T(128)S(1)} %get-tuple-element.98, s32[1024]{0:T(1024)S(1)} %get-tuple-element.96, s32[1024]{0:T(1024)S(1)} %get-tuple-element.95, s32[1024]{0:T(1024)S(1)} %get-tuple-element.94, ...), kind=kLoop, calls=%fused_computation.3 | loop fusion | flops 655360 | bytes 1062144 | tf_op jit(solution)/shard_map/mul | solution.py:501
  127.0 2.2 %collective-permute-start.18 = (bf16[192,640]{1,0:T(8,128)(2,1)S(1)}, bf16[192,640]{1,0:T(8,128)(2,1)S(1)}, u32[]{:S(2)}, u32[]{:S(2)}) collective-permute-start(bf16[192,640]{1,0:T(8,128)(2,1)S(1)} %slice.23), channel_id=1, source_target_pairs={{0,96},{16,112},{32,0},{48,16},{64,32},{80,48},{96,64},{112,80},{1... | collective-permute-start | bytes 737288 | tf_op jit(solution)/shard_map/ppermute | solution.py:40
  129.3 4.2 %collective-permute-start.19 = (f32[8,512]{1,0:T(8,128)S(1)}, f32[8,512]{1,0:T(8,128)S(1)}, u32[]{:S(2)}, u32[]{:S(2)}) collective-permute-start(f32[8,512]{1,0:T(8,128)S(1)} %copy-done.19), channel_id=1, source_target_pairs={{0,128},{128,0},{1,129},{129,1},{2,130},{130,2},{3,131},{131,3},{4... | collective-permute-start | bytes 49160 | tf_op jit(solution)/shard_map/ppermute | solution.py:48
  133.6 4.5 %norm.3 = (bf16[1536,640]{1,0:T(8,128)(2,1)}, bf16[3,64,640]{2,1,0:T(8,128)(2,1)}) custom-call(s32[11]{0:T(128)} %copy-done.9, f32[8,512]{1,0:T(8,128)} %maximum_maximum_fusion.norm_ref.refs_12_, f32[8,2,640]{2,1,0:T(2,128)} %bitcast.40, bf16[512,640]{1,0:T(8,128)(2,1)} %copy-done.12, bf16[512,640]{1,0:T(8,128)(2,1)} %copy-done.13, bf16[512,640]{1,0:T(8,128)(2,1)} %copy-done.14), custom_call_target="tpu_custom_call" | custom-call | flops 1 | bytes 1 | tf_op jit(solution)/shard_map/norm/pallas_call | solution.py:230
  138.2 1.9 %collective-permute-start.21 = (bf16[1536,640]{1,0:T(8,128)(2,1)}, bf16[1536,640]{1,0:T(8,128)(2,1)}, u32[]{:S(2)}, u32[]{:S(2)}) collective-permute-start(bf16[1536,640]{1,0:T(8,128)(2,1)} %get-tuple-element.73.refs_1_), channel_id=1, source_target_pairs={{0,128},{128,0},{1,129},{129,1},{2,130},{130,2},{3,131},{131,3},{4... | collective-permute-start | bytes 5898248 | tf_op jit(solution)/shard_map/ppermute | solution.py:48
  140.7 0.9 copy-done.7
  142.4 2.7 %all-gather.7.cloned.1.call-done = bf16[5120,640]{1,0:T(8,128)(2,1)} async-done(((bf16[640,640]{1,0:T(8,128)(2,1)}), bf16[5120,640]{1,0:T(8,128)(2,1)}) %all-gather.7.cloned.1.call-update) | async-done | bytes 6553616 | tf_op jit(solution)/shard_map/all_gather | solution.py:531
  145.1 0.7 collective-permute-start.25
  146.6 13.9 %project.1 = (f32[1024,640]{1,0:T(8,128)}, f32[8,8,128]{2,1,0:T(8,128)}) custom-call(s32[11]{0:T(128)} %copy-done.9, bf16[2048,640]{1,0:T(8,128)(2,1)} %get-tuple-element.67.refs_0_, bf16[1536,640]{1,0:T(8,128)(2,1)} %get-tuple-element.73.refs_1_, bf16[192,640]{1,0:T(8,128)(2,1)} %copy-done.5, bf16[128,640]{1,0:T(8,128)(2,1)} %copy-done.8, ...), custom_call_target="tpu_custom_call" | custom-call | flops 6710886400 | bytes 19660800 | tf_op jit(solution)/shard_map/project/pallas_call | solution.py:380
  160.5 4.9 %all-to-all-start.2 = ((f32[8,8,128]{2,1,0:T(8,128)}), f32[8,8,128]{2,1,0:T(8,128)S(1)}, u32[]{:S(2)}, u32[]{:S(2)}) async-start(f32[8,8,128]{2,1,0:T(8,128)} %get-tuple-element.82), calls=%async_computation.2 | async-start | bytes 65536 | tf_op jit(solution)/shard_map/all_to_all | solution.py:592
  165.4 0.7 copy-done.18
  166.1 5.0 %turn.1 = (f32[1024,640]{1,0:T(8,128)}, bf16[128,2560]{1,0:T(8,128)(2,1)}) custom-call(s32[11]{0:T(128)} %copy-done.9, f32[1024,640]{1,0:T(8,128)} %get-tuple-element.83.proj_ref, bf16[2,64,2560]{2,1,0:T(8,128)(2,1)} %copy-done, bf16[64,2560]{1,0:T(8,128)(2,1)} %copy-done.18, f32[1,640]{1,0:T(1,128)} %gain_ref.1, f32[1024,128]{1,0:T(8,128)} %get-tuple-element.84.cos_ref, ...), custom_call_target="tpu_custom_call" | custom-call | flops 6553600 | bytes 5898240 | tf_op jit(solution)/shard_map/turn/pallas_call | solution.py:454
  171.4 3.0 %fusion = bf16[1,1,1024,640]{3,2,1,0:T(8,128)(2,1)} fusion(f32[1024,640]{1,0:T(8,128)} %get-tuple-element.87, f32[1024]{0:T(1024)S(1)} %mul.71), kind=kLoop, calls=%fused_computation.1 | loop fusion | flops 1310720 | bytes 3936256 | tf_op jit(solution)/shard_map/broadcast_in_dim | solution.py:602
  (101 shorter events, 4.0 us)
Async XLA Ops:
  7.2 61.2 %all-gather.5.cloned.1.call-start = ((), (), s32[]{:S(2)}) async-start(), calls=%async_computation.3 | async-start | bytes 3686400 | tf_op jit(solution)/shard_map/all_gather | solution.py:531
  7.2 7.7 %collective-permute-start.8 = (bf16[160,640]{1,0:T(8,128)(2,1)}, bf16[160,640]{1,0:T(8,128)(2,1)S(1)}, u32[]{:S(2)}, u32[]{:S(2)}) collective-permute-start(bf16[160,640]{1,0:T(8,128)(2,1)} %param.13), channel_id=1, source_target_pairs={{0,8},{1,9},{2,10},{3,11},{4,12},{5,13},{6,14},{7,15},{8,0},{9,1},... | collective-permute-start | bytes 614408 | tf_op jit(solution)/shard_map/ppermute | solution.py:44
  16.6 35.2 %copy-start.1 = (bf16[1,128,5120]{2,1,0:T(8,128)(2,1)S(1)}, bf16[1,128,5120]{2,1,0:T(8,128)(2,1)}, u32[]{:S(2)}) copy-start(bf16[1,128,5120]{2,1,0:T(8,128)(2,1)} %param.10) | copy-start | bytes 3932164
  16.7 128.4 %all-gather.7.cloned.1.call-start = ((), (), s32[]{:S(2)}) async-start(), calls=%async_computation.4 | async-start | bytes 7372800 | tf_op jit(solution)/shard_map/all_gather | solution.py:531
  16.7 16.5 %collective-permute-start = (bf16[128,2560]{1,0:T(8,128)(2,1)}, bf16[128,2560]{1,0:T(8,128)(2,1)S(1)}, u32[]{:S(2)}, u32[]{:S(2)}) collective-permute-start(bf16[128,2560]{1,0:T(8,128)(2,1)} %bitcast.33), channel_id=1, source_target_pairs={{0,32},{16,48},{32,64},{48,80},{64,96},{80,112},{96,0},{112,16},{1... | collective-permute-start | bytes 1966088 | tf_op jit(solution)/shard_map/ppermute | solution.py:40
  19.0 14.6 %collective-permute-start.1 = (bf16[128,2560]{1,0:T(8,128)(2,1)}, bf16[128,2560]{1,0:T(8,128)(2,1)S(1)}, u32[]{:S(2)}, u32[]{:S(2)}) collective-permute-start(bf16[128,2560]{1,0:T(8,128)(2,1)} %bitcast.34), channel_id=1, source_target_pairs={{0,96},{16,112},{32,0},{48,16},{64,32},{80,48},{96,64},{112,80},{1... | collective-permute-start | bytes 1966088 | tf_op jit(solution)/shard_map/ppermute | solution.py:40
  20.5 10.0 %collective-permute-start.2 = (bf16[320,640]{1,0:T(8,128)(2,1)}, bf16[320,640]{1,0:T(8,128)(2,1)S(1)}, u32[]{:S(2)}, u32[]{:S(2)}) collective-permute-start(bf16[320,640]{1,0:T(8,128)(2,1)} %bitcast.37), channel_id=1, source_target_pairs={{0,8},{1,9},{2,10},{3,11},{4,12},{5,13},{6,14},{7,15},{8,0},{9,1},... | collective-permute-start | bytes 1228808 | tf_op jit(solution)/shard_map/ppermute | solution.py:44
  33.2 20.1 %copy-start.15 = (bf16[128,2560]{1,0:T(8,128)(2,1)}, bf16[128,2560]{1,0:T(8,128)(2,1)S(1)}, u32[]{:S(2)}) copy-start(bf16[128,2560]{1,0:T(8,128)(2,1)S(1)} %collective-permute-done.refs_1_) | copy-start | bytes 1966084
  33.6 19.7 %copy-start.16 = (bf16[128,2560]{1,0:T(8,128)(2,1)}, bf16[128,2560]{1,0:T(8,128)(2,1)S(1)}, u32[]{:S(2)}) copy-start(bf16[128,2560]{1,0:T(8,128)(2,1)S(1)} %collective-permute-done.1.refs_2_) | copy-start | bytes 1966084
  33.6 14.1 %collective-permute-start.4 = (bf16[128,2560]{1,0:T(8,128)(2,1)}, bf16[128,2560]{1,0:T(8,128)(2,1)}, u32[]{:S(2)}, u32[]{:S(2)}) collective-permute-start(bf16[128,2560]{1,0:T(8,128)(2,1)} %bitcast.35), channel_id=1, source_target_pairs={{0,16},{16,0},{32,48},{48,32},{64,80},{80,64},{96,112},{112,96},{1... | collective-permute-start | bytes 1966088 | tf_op jit(solution)/shard_map/ppermute | solution.py:40
  35.2 14.9 %collective-permute-start.3 = (bf16[128,2560]{1,0:T(8,128)(2,1)S(1)}, bf16[128,2560]{1,0:T(8,128)(2,1)}, u32[]{:S(2)}, u32[]{:S(2)}) collective-permute-start(bf16[128,2560]{1,0:T(8,128)(2,1)S(1)} %collective-permute-done.refs_1_), channel_id=1, source_target_pairs={{0,32},{16,48},{32,64},{48,80},{64,96},{80,112},{96,0},{112,16},{1... | collective-permute-start | bytes 1966088 | tf_op jit(solution)/shard_map/ppermute | solution.py:40
  50.1 13.0 %collective-permute-start.5 = (bf16[128,2560]{1,0:T(8,128)(2,1)}, bf16[128,2560]{1,0:T(8,128)(2,1)}, u32[]{:S(2)}, u32[]{:S(2)}) collective-permute-start(bf16[128,2560]{1,0:T(8,128)(2,1)} %collective-permute-done.4.refs_3_), channel_id=1, source_target_pairs={{0,96},{16,112},{32,0},{48,16},{64,32},{80,48},{96,64},{112,80},{1... | collective-permute-start | bytes 1966088 | tf_op jit(solution)/shard_map/ppermute | solution.py:40
  51.2 13.6 %collective-permute-start.6 = (bf16[128,2560]{1,0:T(8,128)(2,1)}, bf16[128,2560]{1,0:T(8,128)(2,1)}, u32[]{:S(2)}, u32[]{:S(2)}) collective-permute-start(bf16[128,2560]{1,0:T(8,128)(2,1)} %collective-permute-done.4.refs_3_), channel_id=1, source_target_pairs={{0,32},{16,48},{32,64},{48,80},{64,96},{80,112},{96,0},{112,16},{1... | collective-permute-start | bytes 1966088 | tf_op jit(solution)/shard_map/ppermute | solution.py:40
  51.6 13.2 %collective-permute-start.7 = (bf16[128,2560]{1,0:T(8,128)(2,1)}, bf16[128,2560]{1,0:T(8,128)(2,1)}, u32[]{:S(2)}, u32[]{:S(2)}) collective-permute-start(bf16[128,2560]{1,0:T(8,128)(2,1)} %collective-permute-done.3.refs_4_), channel_id=1, source_target_pairs={{0,16},{16,0},{32,48},{48,32},{64,80},{80,64},{96,112},{112,96},{1... | collective-permute-start | bytes 1966088 | tf_op jit(solution)/shard_map/ppermute | solution.py:40
  51.8 13.0 %copy-start.9 = (s32[11]{0:T(128)}, s32[11]{0:T(128)S(1)}, u32[]{:S(2)}) copy-start(s32[11]{0:T(128)S(1)} %stack.47.where_ref) | copy-start | bytes 136
  64.8 13.6 %all-to-all-start = ((bf16[8,64,640]{2,1,0:T(8,128)(2,1)}), bf16[8,64,640]{2,1,0:T(8,128)(2,1)S(1)}, u32[]{:S(2)}, u32[]{:S(2)}) async-start(bf16[8,64,640]{2,1,0:T(8,128)(2,1)} %split_columns.1), calls=%async_computation | async-start | bytes 1310720 | tf_op jit(solution)/shard_map/all_to_all | solution.py:543
  68.4 15.2 %copy-start.20 = (f32[640]{0:T(1024)S(1)}, f32[640]{0:T(1024)}, u32[]{:S(2)}) copy-start(f32[640]{0:T(1024)} %param.14) | copy-start | bytes 7684
  68.4 18.1 %copy-start.11 = (s32[1,128]{1,0:T(1,128)S(1)}, s32[1,128]{1,0:T(1,128)}, u32[]{:S(2)}) copy-start(s32[1,128]{1,0:T(1,128)} %cell_ref.1) | copy-start | bytes 1540
  78.3 8.1 %collective-permute-start.9 = (f32[512,640]{1,0:T(8,128)}, f32[512,640]{1,0:T(8,128)S(1)}, u32[]{:S(2)}, u32[]{:S(2)}) collective-permute-start(f32[512,640]{1,0:T(8,128)} %get-tuple-element.59), channel_id=1, source_target_pairs={{0,128},{128,0},{1,129},{129,1},{2,130},{130,2},{3,131},{131,3},{4... | collective-permute-start | bytes 3932168 | tf_op jit(solution)/shard_map/ppermute | solution.py:48
  89.1 25.4 %copy-start.3 = (bf16[512,640]{1,0:T(8,128)(2,1)}, bf16[512,640]{1,0:T(8,128)(2,1)S(1)}, u32[]{:S(2)}) copy-start(bf16[512,640]{1,0:T(8,128)(2,1)S(1)} %get-tuple-element.61.refs_0_) | copy-start | bytes 1966084
  89.1 19.9 %collective-permute-start.10 = (bf16[512,640]{1,0:T(8,128)(2,1)S(1)}, bf16[512,640]{1,0:T(8,128)(2,1)}, u32[]{:S(2)}, u32[]{:S(2)}) collective-permute-start(bf16[512,640]{1,0:T(8,128)(2,1)S(1)} %get-tuple-element.61.refs_0_), channel_id=1, source_target_pairs={{0,32},{16,48},{32,64},{48,80},{64,96},{80,112},{96,0},{112,16},{1... | collective-permute-start | bytes 1966088 | tf_op jit(solution)/shard_map/ppermute | solution.py:40
  90.8 18.2 %collective-permute-start.11 = (bf16[512,640]{1,0:T(8,128)(2,1)S(1)}, bf16[512,640]{1,0:T(8,128)(2,1)S(1)}, u32[]{:S(2)}, u32[]{:S(2)}) collective-permute-start(bf16[512,640]{1,0:T(8,128)(2,1)S(1)} %get-tuple-element.61.refs_0_), channel_id=1, source_target_pairs={{0,96},{16,112},{32,0},{48,16},{64,32},{80,48},{96,64},{112,80},{1... | collective-permute-start | bytes 1966088 | tf_op jit(solution)/shard_map/ppermute | solution.py:40
  92.1 17.8 %collective-permute-start.12 = (bf16[512,640]{1,0:T(8,128)(2,1)S(1)}, bf16[512,640]{1,0:T(8,128)(2,1)}, u32[]{:S(2)}, u32[]{:S(2)}) collective-permute-start(bf16[512,640]{1,0:T(8,128)(2,1)S(1)} %get-tuple-element.61.refs_0_), channel_id=1, source_target_pairs={{0,16},{16,0},{32,48},{48,32},{64,80},{80,64},{96,112},{112,96},{1... | collective-permute-start | bytes 1966088 | tf_op jit(solution)/shard_map/ppermute | solution.py:40
  93.6 15.4 %all-to-all-start.1 = ((f32[8,16,128]{2,1,0:T(8,128)}), f32[8,16,128]{2,1,0:T(8,128)S(1)}, u32[]{:S(2)}, u32[]{:S(2)}) async-start(f32[8,16,128]{2,1,0:T(8,128)} %get-tuple-element.62), calls=%async_computation.1 | async-start | bytes 131072 | tf_op jit(solution)/shard_map/all_to_all | solution.py:556
  109.8 16.7 %collective-permute-start.13 = (bf16[512,640]{1,0:T(8,128)(2,1)}, bf16[512,640]{1,0:T(8,128)(2,1)S(1)}, u32[]{:S(2)}, u32[]{:S(2)}) collective-permute-start(bf16[512,640]{1,0:T(8,128)(2,1)} %collective-permute-done.10.refs_1_), channel_id=1, source_target_pairs={{0,32},{16,48},{32,64},{48,80},{64,96},{80,112},{96,0},{112,16},{1... | collective-permute-start | bytes 1966088 | tf_op jit(solution)/shard_map/ppermute | solution.py:40
  110.5 16.1 %collective-permute-start.15 = (bf16[512,640]{1,0:T(8,128)(2,1)}, bf16[512,640]{1,0:T(8,128)(2,1)S(1)}, u32[]{:S(2)}, u32[]{:S(2)}) collective-permute-start(bf16[512,640]{1,0:T(8,128)(2,1)} %collective-permute-done.10.refs_1_), channel_id=1, source_target_pairs={{0,16},{16,0},{32,48},{48,32},{64,80},{80,64},{96,112},{112,96},{1... | collective-permute-start | bytes 1966088 | tf_op jit(solution)/shard_map/ppermute | solution.py:40
  111.6 15.0 %collective-permute-start.14 = (bf16[512,640]{1,0:T(8,128)(2,1)}, bf16[512,640]{1,0:T(8,128)(2,1)S(1)}, u32[]{:S(2)}, u32[]{:S(2)}) collective-permute-start(bf16[512,640]{1,0:T(8,128)(2,1)} %collective-permute-done.12.refs_3_), channel_id=1, source_target_pairs={{0,96},{16,112},{32,0},{48,16},{64,32},{80,48},{96,64},{112,80},{1... | collective-permute-start | bytes 1966088 | tf_op jit(solution)/shard_map/ppermute | solution.py:40
  119.8 9.5 %copy-start.19 = (f32[8,512]{1,0:T(8,128)S(1)}, f32[8,512]{1,0:T(8,128)}, u32[]{:S(2)}) copy-start(f32[8,512]{1,0:T(8,128)} %maximum_maximum_fusion.norm_ref.refs_12_) | copy-start | bytes 49156
  119.8 26.0 %collective-permute-start.20 = (bf16[2048,640]{1,0:T(8,128)(2,1)}, bf16[2048,640]{1,0:T(8,128)(2,1)}, u32[]{:S(2)}, u32[]{:S(2)}) collective-permute-start(bf16[2048,640]{1,0:T(8,128)(2,1)} %get-tuple-element.67.refs_0_), channel_id=1, source_target_pairs={{0,128},{128,0},{1,129},{129,1},{2,130},{130,2},{3,131},{131,3},{4... | collective-permute-start | bytes 7864328 | tf_op jit(solution)/shard_map/ppermute | solution.py:48
  126.6 7.0 %copy-start.12 = (bf16[512,640]{1,0:T(8,128)(2,1)}, bf16[512,640]{1,0:T(8,128)(2,1)S(1)}, u32[]{:S(2)}) copy-start(bf16[512,640]{1,0:T(8,128)(2,1)S(1)} %collective-permute-done.13.refs_0_) | copy-start | bytes 1966084
  126.6 7.0 %copy-start.13 = (bf16[512,640]{1,0:T(8,128)(2,1)}, bf16[512,640]{1,0:T(8,128)(2,1)S(1)}, u32[]{:S(2)}) copy-start(bf16[512,640]{1,0:T(8,128)(2,1)S(1)} %collective-permute-done.14.refs_1_) | copy-start | bytes 1966084
  126.6 14.1 %copy-start.4 = (bf16[4,64,640]{2,1,0:T(8,128)(2,1)S(1)}, bf16[4,64,640]{2,1,0:T(8,128)(2,1)}, u32[]{:S(2)}) copy-start(bf16[4,64,640]{2,1,0:T(8,128)(2,1)} %get-tuple-element.78.first_ref) | copy-start | bytes 983044
  126.6 14.1 %copy-start.10 = (s32[11]{0:T(128)S(1)}, s32[11]{0:T(128)}, u32[]{:S(2)}) copy-start(s32[11]{0:T(128)} %copy-done.9) | copy-start | bytes 136
  126.7 11.5 %collective-permute-start.16 = (bf16[192,640]{1,0:T(8,128)(2,1)S(1)}, bf16[192,640]{1,0:T(8,128)(2,1)S(1)}, u32[]{:S(2)}, u32[]{:S(2)}) collective-permute-start(bf16[192,640]{1,0:T(8,128)(2,1)S(1)} %slice.21), channel_id=1, source_target_pairs={{0,16},{16,0},{32,48},{48,32},{64,80},{80,64},{96,112},{112,96},{1... | collective-permute-start | bytes 737288 | tf_op jit(solution)/shard_map/ppermute | solution.py:40
  127.0 11.2 %collective-permute-start.18 = (bf16[192,640]{1,0:T(8,128)(2,1)S(1)}, bf16[192,640]{1,0:T(8,128)(2,1)S(1)}, u32[]{:S(2)}, u32[]{:S(2)}) collective-permute-start(bf16[192,640]{1,0:T(8,128)(2,1)S(1)} %slice.23), channel_id=1, source_target_pairs={{0,96},{16,112},{32,0},{48,16},{64,32},{80,48},{96,64},{112,80},{1... | collective-permute-start | bytes 737288 | tf_op jit(solution)/shard_map/ppermute | solution.py:40
  129.2 8.9 %collective-permute-start.17 = (bf16[128,640]{1,0:T(8,128)(2,1)S(1)}, bf16[128,640]{1,0:T(8,128)(2,1)S(1)}, u32[]{:S(2)}, u32[]{:S(2)}) collective-permute-start(bf16[128,640]{1,0:T(8,128)(2,1)S(1)} %slice.22), channel_id=1, source_target_pairs={{0,32},{16,48},{32,64},{48,80},{64,96},{80,112},{96,0},{112,16},{1... | collective-permute-start | bytes 491528 | tf_op jit(solution)/shard_map/ppermute | solution.py:40
  129.3 8.8 %collective-permute-start.19 = (f32[8,512]{1,0:T(8,128)S(1)}, f32[8,512]{1,0:T(8,128)S(1)}, u32[]{:S(2)}, u32[]{:S(2)}) collective-permute-start(f32[8,512]{1,0:T(8,128)S(1)} %copy-done.19), channel_id=1, source_target_pairs={{0,128},{128,0},{1,129},{129,1},{2,130},{130,2},{3,131},{131,3},{4... | collective-permute-start | bytes 49160 | tf_op jit(solution)/shard_map/ppermute | solution.py:48
  138.1 7.7 %copy-start.24 = (f32[8,512]{1,0:T(8,128)}, f32[8,512]{1,0:T(8,128)S(1)}, u32[]{:S(2)}) copy-start(f32[8,512]{1,0:T(8,128)S(1)} %collective-permute-done.19.refs_13_) | copy-start | bytes 49156
  138.1 7.7 %copy-start.8 = (bf16[128,640]{1,0:T(8,128)(2,1)}, bf16[128,640]{1,0:T(8,128)(2,1)S(1)}, u32[]{:S(2)}) copy-start(bf16[128,640]{1,0:T(8,128)(2,1)S(1)} %collective-permute-done.17.refs_1_.refs_3_) | copy-start | bytes 491524
  138.2 7.7 %copy-start.5 = (bf16[192,640]{1,0:T(8,128)(2,1)}, bf16[192,640]{1,0:T(8,128)(2,1)S(1)}, u32[]{:S(2)}) copy-start(bf16[192,640]{1,0:T(8,128)(2,1)S(1)} %collective-permute-done.16.refs_0_.refs_2_) | copy-start | bytes 737284
  138.2 7.7 %copy-start.6 = (bf16[192,640]{1,0:T(8,128)(2,1)}, bf16[192,640]{1,0:T(8,128)(2,1)S(1)}, u32[]{:S(2)}) copy-start(bf16[192,640]{1,0:T(8,128)(2,1)S(1)} %collective-permute-done.18.refs_2_.refs_4_) | copy-start | bytes 737284
  138.2 7.6 %collective-permute-start.21 = (bf16[1536,640]{1,0:T(8,128)(2,1)}, bf16[1536,640]{1,0:T(8,128)(2,1)}, u32[]{:S(2)}, u32[]{:S(2)}) collective-permute-start(bf16[1536,640]{1,0:T(8,128)(2,1)} %get-tuple-element.73.refs_1_), channel_id=1, source_target_pairs={{0,128},{128,0},{1,129},{129,1},{2,130},{130,2},{3,131},{131,3},{4... | collective-permute-start | bytes 5898248 | tf_op jit(solution)/shard_map/ppermute | solution.py:48
  140.1 5.7 %collective-permute-start.22 = (bf16[192,640]{1,0:T(8,128)(2,1)S(1)}, bf16[192,640]{1,0:T(8,128)(2,1)S(1)}, u32[]{:S(2)}, u32[]{:S(2)}) collective-permute-start(bf16[192,640]{1,0:T(8,128)(2,1)S(1)} %collective-permute-done.16.refs_0_.refs_2_), channel_id=1, source_target_pairs={{0,128},{128,0},{1,129},{129,1},{2,130},{130,2},{3,131},{131,3},{4... | collective-permute-start | bytes 737288 | tf_op jit(solution)/shard_map/ppermute | solution.py:48
  140.2 5.6 %collective-permute-start.24 = (bf16[192,640]{1,0:T(8,128)(2,1)S(1)}, bf16[192,640]{1,0:T(8,128)(2,1)S(1)}, u32[]{:S(2)}, u32[]{:S(2)}) collective-permute-start(bf16[192,640]{1,0:T(8,128)(2,1)S(1)} %collective-permute-done.18.refs_2_.refs_4_), channel_id=1, source_target_pairs={{0,128},{128,0},{1,129},{129,1},{2,130},{130,2},{3,131},{131,3},{4... | collective-permute-start | bytes 737288 | tf_op jit(solution)/shard_map/ppermute | solution.py:48
  140.6 4.5 %collective-permute-start.23 = (bf16[128,640]{1,0:T(8,128)(2,1)S(1)}, bf16[128,640]{1,0:T(8,128)(2,1)S(1)}, u32[]{:S(2)}, u32[]{:S(2)}) collective-permute-start(bf16[128,640]{1,0:T(8,128)(2,1)S(1)} %collective-permute-done.17.refs_1_.refs_3_), channel_id=1, source_target_pairs={{0,128},{128,0},{1,129},{129,1},{2,130},{130,2},{3,131},{131,3},{4... | collective-permute-start | bytes 491528 | tf_op jit(solution)/shard_map/ppermute | solution.py:48
  142.3 18.1 %copy-start = (bf16[2,64,2560]{2,1,0:T(8,128)(2,1)}, bf16[2,64,2560]{2,1,0:T(8,128)(2,1)S(1)}, u32[]{:S(2)}) copy-start(bf16[2,64,2560]{2,1,0:T(8,128)(2,1)S(1)} %next_rows.1.next_ref) | copy-start | bytes 1966084
  145.1 20.3 %collective-permute-start.25 = (bf16[64,2560]{1,0:T(8,128)(2,1)S(1)}, bf16[64,2560]{1,0:T(8,128)(2,1)S(1)}, u32[]{:S(2)}, u32[]{:S(2)}) collective-permute-start(bf16[64,2560]{1,0:T(8,128)(2,1)S(1)} %dynamic-slice_bitcast_fusion), channel_id=1, source_target_pairs={{0,128},{128,0},{1,129},{129,1},{2,130},{130,2},{3,131},{131,3},{4... | collective-permute-start | bytes 983048 | tf_op jit(solution)/shard_map/ppermute | solution.py:48
  160.5 10.7 %all-to-all-start.2 = ((f32[8,8,128]{2,1,0:T(8,128)}), f32[8,8,128]{2,1,0:T(8,128)S(1)}, u32[]{:S(2)}, u32[]{:S(2)}) async-start(f32[8,8,128]{2,1,0:T(8,128)} %get-tuple-element.82), calls=%async_computation.2 | async-start | bytes 65536 | tf_op jit(solution)/shard_map/all_to_all | solution.py:592
  (8 other events, 13.1 us)
Sparse Core Ops, SparseCore 0:
  16.8 50.9 all-gather.4
  69.5 75.5 all-gather.6
